TPU v7x, 32 devices: a whole 2x2x4 slice. The times are simulated.
32 devices in a mesh: gx: 8 (over z, core), yz: 4 (over y, x).
Axes of the slice: x: 2, y: 2, z: 4, core: 2. Of those that a mesh axis runs over, the one named last changes fastest.
Arguments:
- gauge_links: float32 [16, 2, 3, 3, 512], P('gx', None, None, None, 'yz'), may hold values from -1 to 1, as said below
- in_field: float32 [8, 16, 2, 3, 3, 512], P(None, 'gx', None, None, None, 'yz'), may hold values from -6 to 6
- cotangent: float32 [8, 16, 2, 3, 3, 512], P(None, 'gx', None, None, None, 'yz'), may hold values from -6 to 6
- bilinear_weights: float32 [8, 8, 8, 8], replicated, may hold values from -0.25 to 0.25
Outputs:
- grad_field: float32 [8, 16, 2, 3, 3, 512], P(None, 'gx', None, None, None, 'yz')
- grad_weights: float32 [8, 8, 8, 8], replicated
Inputs may be any that keep to these rules, and one draw needn't show every extreme that they name: `gauge_links`: every site's link is a special unitary 3 x 3 matrix (unitary with determinant 1), stored as real and imaginary parts.
All inputs are finite; a program needn't handle non-finite values.
Results may differ from a plain program's by a relative error of at most 0.0003.
Values sent between devices are 32-bit elements; how exact they have to be, the bound alone decides.
A program may use at most 64 MiB of HBM per device.

v0:
```python
import math

import jax
import jax.numpy as jnp
from jax import lax
from jax.sharding import PartitionSpec as P


def from_behind(block, axis, distance):
    devices = range(lax.axis_size(axis))
    route = [((i - distance) % len(devices), i) for i in devices]
    return lax.ppermute(block, axis, route)


def matmul_three(left, right):
    return jnp.sum(left[..., :, :, None, :] * right[..., None, :, :, :], axis=-3)


def complex_mul(left, right):
    left_re = left[..., 0, :, :, :]
    left_im = left[..., 1, :, :, :]
    right_re = right[..., 0, :, :, :]
    right_im = right[..., 1, :, :, :]
    real_part = matmul_three(left_re, right_re) - matmul_three(left_im, right_im)
    imag_part = matmul_three(left_re, right_im) + matmul_three(left_im, right_re)
    return jnp.stack([real_part, imag_part], axis=-4)


def dagger(matrix):
    swapped = jnp.swapaxes(matrix, -3, -2)
    return jnp.stack([swapped[..., 0, :, :, :], -swapped[..., 1, :, :, :]], axis=-4)


def per_device(gauge_links, in_field, cotangent, bilinear_weights):
    part_x = gauge_links.shape[0]
    channels = in_field.shape[0]
    line_count = bilinear_weights.shape[2]
    site_count = gauge_links.shape[-1]
    reach_devs = (part_x - 1 + line_count) // part_x
    highest = lax.Precision.HIGHEST
    weight_rows = bilinear_weights.reshape(channels * channels, line_count * channels)

    def advance(carry, unused):
        arrived = from_behind(carry, "gx", -1)
        return (arrived, arrived)

    unused_last, stacked = lax.scan(advance, (gauge_links, in_field), None, length=reach_devs)
    window_links = jnp.concatenate(
        [gauge_links, stacked[0].reshape((-1, 2, 3, 3, site_count))], axis=0
    )
    later_field = jnp.moveaxis(stacked[1], 0, 1).reshape((channels, -1, 2, 3, 3, site_count))
    window_field = jnp.concatenate([in_field, later_field], axis=1)
    pair_grad = complex_mul(dagger(in_field)[None], cotangent[:, None]).reshape(
        channels * channels, -1
    )

    def forward_step(line, offset):
        shifted = lax.dynamic_slice_in_dim(window_field, offset, part_x, axis=1)
        transported = complex_mul(complex_mul(line[None], shifted), dagger(line)[None])
        next_links = lax.dynamic_slice_in_dim(window_links, offset, part_x, axis=0)
        return (complex_mul(line, next_links), (transported, line))

    offsets = jnp.arange(1, line_count + 1, dtype=jnp.int32)
    unused_line, (all_transported, all_lines) = lax.scan(forward_step, gauge_links, offsets)
    transported_flat = all_transported.reshape(line_count * channels, -1)
    partial_grad = lax.dot_general(
        pair_grad, transported_flat, (((1,), (1,)), ((), ())), precision=highest
    )
    mixed = jnp.dot(weight_rows, transported_flat, precision=highest)
    mixed_matrix = mixed.reshape((channels, channels) + in_field.shape[1:])
    direct = jnp.sum(complex_mul(cotangent[:, None], dagger(mixed_matrix)), axis=0)
    line_grad = jnp.dot(weight_rows.T, pair_grad, precision=highest)
    line_grad = line_grad.reshape((line_count,) + in_field.shape)
    accumulator = jnp.zeros((channels, (reach_devs + 1) * part_x, 2, 3, 3, site_count), jnp.float32)

    def backward_step(carry, inputs):
        offset, grad_piece, line = inputs
        contribution = complex_mul(complex_mul(dagger(line)[None], grad_piece), line[None])
        current = lax.dynamic_slice_in_dim(carry, offset, part_x, axis=1)
        return (
            lax.dynamic_update_slice_in_dim(carry, current + contribution, offset, axis=1),
            None,
        )

    accumulator, unused_out = lax.scan(backward_step, accumulator, (offsets, line_grad, all_lines))
    block_count = reach_devs + 1
    half_span = 1 << reach_devs.bit_length() - 1
    pending = accumulator
    while half_span >= 1:
        moving = pending[:, half_span * part_x : block_count * part_x]
        arrived = from_behind(moving, "gx", half_span)
        kept_count = block_count - half_span
        updated = pending[:, : kept_count * part_x] + arrived
        pending = jnp.concatenate(
            [updated, pending[:, kept_count * part_x : half_span * part_x]], axis=1
        )
        block_count = half_span
        half_span = half_span // 2
    grad_field = direct + pending
    total_x = part_x * lax.axis_size("gx")
    total_sites = site_count * lax.axis_size("yz")
    summed = lax.psum(partial_grad, ("gx", "yz"))
    grad_weights = summed.reshape(channels, channels, line_count, channels) / math.sqrt(
        100.0 * total_x * total_sites
    )
    return (grad_field, grad_weights)


def solution(mesh):
    placed = (
        P("gx", None, None, None, "yz"),
        P(None, "gx", None, None, None, "yz"),
        P(None, "gx", None, None, None, "yz"),
        P(),
    )
    return jax.shard_map(
        per_device,
        mesh=mesh,
        in_specs=placed,
        out_specs=(P(None, "gx", None, None, None, "yz"), P()),
        check_vma=False,
    )
```

profile of v0, /device:TPU:0, one launch (start us, length us, event | category | flops | bytes accessed | tf_op | source)
XLA Modules:
  0.0 152.9 jit_solution(12746494167958758216)
XLA Ops:
  0.6 0.7 copy.187
  1.4 0.9 copy.188
  2.3 28.2 %while.40 = (s32[]{:T(128)}, f32[2,2,3,3,128]{4,1,3,2,0:T(2,128)S(1)}, f32[8,2,2,3,3,128]{5,2,4,3,1,0:T(2,128)S(1)}, f32[4,2,2,3,3,128]{5,1,0,4,3,2:T(2,128)S(1)...) while((s32[]{:T(128)}, f32[2,2,3,3,128]{4,1,3,2,0:T(2,128)S(1)}, ...), condition=%wide.region_1.2_spmd, body=%wide.region_0.1_spmd.sunk | while | flops 2 | bytes 1327269 | solution.py:47
  2.4 4.5 %collective-permute-start = (f32[2,2,3,3,128]{4,1,3,2,0:T(2,128)S(1)}, f32[2,2,3,3,128]{4,1,3,2,0:T(2,128)S(1)}, u32[]{:S(2)}, u32[]{:S(2)}) collective-permute-start(f32[2,2,3,3,128]{4,1,3,2,0:T(2,128)S(1)} %get-tuple-element.454), channel_id=1, source_target_pairs={{4,0},{8,4},{12,8},{16,12},{20,16},{24,20},{28,24},{0,28},{5,1},{9... | collective-permute-start | bytes 55304 | tf_op jit(solution)/shard_map/while/body/eval_jaxpr/ppermute | solution.py:12
  6.9 0.7 collective-permute-start.1
  7.6 0.8 collective-permute-done
  8.4 1.9 %collective-permute-done.1 = f32[8,2,2,3,3,128]{5,2,4,3,1,0:T(2,128)S(1)} collective-permute-done((f32[8,2,2,3,3,128]{5,2,4,3,1,0:T(2,128)S(1)}, f32[8,2,2,3,3,128]{5,2,4,3,1,0:T(2,128)S(1)}, u32[]{:S(2)}, u32[]{:S(2)}) %collective-permute-start.1) | collective-permute-done | bytes 147488 | tf_op jit(solution)/shard_map/while/body/eval_jaxpr/ppermute | solution.py:12
  10.4 3.7 %collective-permute-start = (f32[2,2,3,3,128]{4,1,3,2,0:T(2,128)S(1)}, f32[2,2,3,3,128]{4,1,3,2,0:T(2,128)S(1)}, u32[]{:S(2)}, u32[]{:S(2)}) collective-permute-start(f32[2,2,3,3,128]{4,1,3,2,0:T(2,128)S(1)} %get-tuple-element.454), channel_id=1, source_target_pairs={{4,0},{8,4},{12,8},{16,12},{20,16},{24,20},{28,24},{0,28},{5,1},{9... | collective-permute-start | bytes 55304 | tf_op jit(solution)/shard_map/while/body/eval_jaxpr/ppermute | solution.py:12
  14.2 1.4 collective-permute-done
  15.6 1.4 collective-permute-done.1
  17.1 3.8 %collective-permute-start = (f32[2,2,3,3,128]{4,1,3,2,0:T(2,128)S(1)}, f32[2,2,3,3,128]{4,1,3,2,0:T(2,128)S(1)}, u32[]{:S(2)}, u32[]{:S(2)}) collective-permute-start(f32[2,2,3,3,128]{4,1,3,2,0:T(2,128)S(1)} %get-tuple-element.454), channel_id=1, source_target_pairs={{4,0},{8,4},{12,8},{16,12},{20,16},{24,20},{28,24},{0,28},{5,1},{9... | collective-permute-start | bytes 55304 | tf_op jit(solution)/shard_map/while/body/eval_jaxpr/ppermute | solution.py:12
  20.9 1.4 collective-permute-done
  22.3 1.4 collective-permute-done.1
  23.8 3.8 %collective-permute-start = (f32[2,2,3,3,128]{4,1,3,2,0:T(2,128)S(1)}, f32[2,2,3,3,128]{4,1,3,2,0:T(2,128)S(1)}, u32[]{:S(2)}, u32[]{:S(2)}) collective-permute-start(f32[2,2,3,3,128]{4,1,3,2,0:T(2,128)S(1)} %get-tuple-element.454), channel_id=1, source_target_pairs={{4,0},{8,4},{12,8},{16,12},{20,16},{24,20},{28,24},{0,28},{5,1},{9... | collective-permute-start | bytes 55304 | tf_op jit(solution)/shard_map/while/body/eval_jaxpr/ppermute | solution.py:12
  27.6 1.4 collective-permute-done
  29.1 1.4 collective-permute-done.1
  30.7 26.4 %while.41 = (s32[]{:T(128)}, f32[2,2,3,3,128]{4,0,3,2,1:T(2,128)S(1)}, f32[8,8,2,2,3,3,128]{6,1,5,4,3,2,0:T(8,128)S(1)}, f32[8,2,2,3,3,128]{5,1,4,3,2,0:T(2,128)...) while((s32[]{:T(128)}, ...), condition=%wide.region_15.16_spmd, body=%wide.region_2.15_spmd.sunk | while | flops 910086 | bytes 2894015 | solution.py:64
  30.7 0.7 dynamic_slice.34
  34.0 0.7 dynamic_slice.34
  37.3 0.7 dynamic_slice.34
  40.6 0.7 dynamic_slice.34
  43.9 0.7 dynamic_slice.34
  47.2 0.7 dynamic_slice.34
  50.5 0.7 dynamic_slice.34
  53.8 0.7 dynamic_slice.34
  57.2 1.2 fusion.6
  58.6 0.8 copy-done.4
  59.4 3.8 %multiply_reduce_fusion.27 = (f32[8,8,2,3,3,128]{5,1,4,3,2,0:T(8,128)}, f32[8,8,2,3,3,128]{5,1,4,3,2,0:T(8,128)}, f32[8,8,2,3,3,128]{5,1,4,3,2,0:T(8,128)}, f32[...) fusion(f32[8,2,3,3,128]{4,3,2,1,0:T(4,128)S(1)} %copy.63, ...), kind=kLoop, calls=%fused_computation.66 | loop fusion | flops 5898240 | bytes 6193152 | tf_op jit(solution)/shard_map/reduce_sum | solution.py:16
  63.5 2.2 %fusion.7 = f32[4608,64]{0,1:T(8,128)} fusion(f32[64,4608]{1,0:T(8,128)S(1)} %bitcast.160, f32[64,64]{1,0:T(8,128)S(1)} %reshape.181), kind=kOutput, calls=%fused_computation.97 | convolution fusion | flops 226492416 | bytes 2375680 | tf_op jit(solution)/shard_map/dot_general | solution.py:72
  65.8 31.2 %while.42 = (s32[]{:T(128)}, f32[8,10,2,3,3,128]{5,0,4,3,2,1:T(8,128)S(1)}, s32[8]{0:T(128)S(1)}, f32[8,2,2,3,3,128]{5,1,4,3,2,0:T(2,128)S(1)}, f32[8,8,2,2,3,3,...) while((s32[]{:T(128)}, f32[8,10,2,3,3,128]{5,0,4,3,2,1:T(8,128)S(1)}, s32[8]{0:T(128)S(1)}, ...), condition=%wide.region_34.35_spmd, body=%wide.region_25.34_spmd.sunk | while | flops 891653 | bytes 3410575 | solution.py:85
  65.9 0.9 copy_bitcast_fusion.7
  67.1 0.6 dynamic_slice.38
  69.8 0.9 copy_bitcast_fusion.7
  73.7 0.9 copy_bitcast_fusion.7
  77.6 0.9 copy_bitcast_fusion.7
  81.5 0.9 copy_bitcast_fusion.7
  85.4 0.9 copy_bitcast_fusion.7
  89.3 0.9 copy_bitcast_fusion.7
  93.2 0.9 copy_bitcast_fusion.7
  94.4 0.6 dynamic_slice.38
  97.0 0.7 slice.117
  98.1 2.6 %add_bitcast_fusion.4 = (f32[8,8,2,1,3,3,128]{6,1,5,4,2,0,3:T(8,128)}, f32[8,8,2,1,3,3,128]{6,1,5,4,2,0,3:T(8,128)}) fusion(f32[8,8,2,3,3,128]{5,1,4,3,2,0:T(8,128)} %get-tuple-element.170, f32[8,8,2,3,3,128]{5,1,4,3,2,0:T(8,128)} %get-tuple-element.169, f32[8,8,2,3,3,128]{5,1,4,3,2,0:T(8,128)S(1)} %copy-done, f32[8,8,2,3,3,128]{5,1,4,3,2,0:T(8,128)} %get-tuple-element.171), kind=kLoop, calls=%fused_computation.75 | loop fusion | flops 294912 | bytes 3538944 | tf_op jit(solution)/shard_map/add | solution.py:25
  100.7 1.7 %fusion.8 = f32[64,64]{1,0:T(8,128)} fusion(f32[64,4608]{1,0:T(8,128)S(1)} %bitcast.161, f32[64,4608]{1,0:T(8,128)S(1)} %bitcast.165), kind=kOutput, calls=%fused_computation.98 | convolution fusion | flops 226492416 | bytes 2375680 | tf_op jit(solution)/shard_map/dot_general | solution.py:66
  102.5 42.1 %psum.7 = f32[64,64]{1,0:T(8,128)S(1)} all-reduce(f32[64,64]{1,0:T(8,128)} %fusion.8), channel_id=1, replica_groups=mesh['gx'=8,'yz'=4] {'gx','yz'}, use_global_device_ids=true, to_apply=%region_35.36 | all-reduce | flops 4096 | bytes 32768 | tf_op jit(solution)/shard_map/psum | solution.py:102
  144.7 1.0 fusion.1
  145.8 0.8 div.10
  146.7 5.4 %collective-permute-done.4 = f32[8,2,2,3,3,128]{5,0,4,3,2,1:T(8,128)S(1)} collective-permute-done((f32[8,2,2,3,3,128]{5,0,4,3,2,1:T(8,128)S(1)}, f32[8,2,2,3,3,128]{5,0,4,3,2,1:T(8,128)S(1)}, u32[]{:S(2)}, u32[]{:S(2)}) %collective-permute-start.4) | collective-permute-done | bytes 147488 | tf_op jit(solution)/shard_map/ppermute | solution.py:12
  152.1 0.7 copy.84
  (374 shorter events, 11.3 us)
Async XLA Ops:
  2.4 6.0 %collective-permute-start = (f32[2,2,3,3,128]{4,1,3,2,0:T(2,128)S(1)}, f32[2,2,3,3,128]{4,1,3,2,0:T(2,128)S(1)}, u32[]{:S(2)}, u32[]{:S(2)}) collective-permute-start(f32[2,2,3,3,128]{4,1,3,2,0:T(2,128)S(1)} %get-tuple-element.454), channel_id=1, source_target_pairs={{4,0},{8,4},{12,8},{16,12},{20,16},{24,20},{28,24},{0,28},{5,1},{9... | collective-permute-start | bytes 55304 | tf_op jit(solution)/shard_map/while/body/eval_jaxpr/ppermute | solution.py:12
  6.9 3.4 %collective-permute-start.1 = (f32[8,2,2,3,3,128]{5,2,4,3,1,0:T(2,128)S(1)}, f32[8,2,2,3,3,128]{5,2,4,3,1,0:T(2,128)S(1)}, u32[]{:S(2)}, u32[]{:S(2)}) collective-permute-start(f32[8,2,2,3,3,128]{5,2,4,3,1,0:T(2,128)S(1)} %get-tuple-element.455), channel_id=1, source_target_pairs={{4,0},{8,4},{12,8},{16,12},{20,16},{24,20},{28,24},{0,28},{5,1},{9... | collective-permute-start | bytes 442376 | tf_op jit(solution)/shard_map/while/body/eval_jaxpr/ppermute | solution.py:12
  10.4 5.2 %collective-permute-start = (f32[2,2,3,3,128]{4,1,3,2,0:T(2,128)S(1)}, f32[2,2,3,3,128]{4,1,3,2,0:T(2,128)S(1)}, u32[]{:S(2)}, u32[]{:S(2)}) collective-permute-start(f32[2,2,3,3,128]{4,1,3,2,0:T(2,128)S(1)} %get-tuple-element.454), channel_id=1, source_target_pairs={{4,0},{8,4},{12,8},{16,12},{20,16},{24,20},{28,24},{0,28},{5,1},{9... | collective-permute-start | bytes 55304 | tf_op jit(solution)/shard_map/while/body/eval_jaxpr/ppermute | solution.py:12
  14.1 2.9 %collective-permute-start.1 = (f32[8,2,2,3,3,128]{5,2,4,3,1,0:T(2,128)S(1)}, f32[8,2,2,3,3,128]{5,2,4,3,1,0:T(2,128)S(1)}, u32[]{:S(2)}, u32[]{:S(2)}) collective-permute-start(f32[8,2,2,3,3,128]{5,2,4,3,1,0:T(2,128)S(1)} %get-tuple-element.455), channel_id=1, source_target_pairs={{4,0},{8,4},{12,8},{16,12},{20,16},{24,20},{28,24},{0,28},{5,1},{9... | collective-permute-start | bytes 442376 | tf_op jit(solution)/shard_map/while/body/eval_jaxpr/ppermute | solution.py:12
  17.1 5.2 %collective-permute-start = (f32[2,2,3,3,128]{4,1,3,2,0:T(2,128)S(1)}, f32[2,2,3,3,128]{4,1,3,2,0:T(2,128)S(1)}, u32[]{:S(2)}, u32[]{:S(2)}) collective-permute-start(f32[2,2,3,3,128]{4,1,3,2,0:T(2,128)S(1)} %get-tuple-element.454), channel_id=1, source_target_pairs={{4,0},{8,4},{12,8},{16,12},{20,16},{24,20},{28,24},{0,28},{5,1},{9... | collective-permute-start | bytes 55304 | tf_op jit(solution)/shard_map/while/body/eval_jaxpr/ppermute | solution.py:12
  20.8 2.9 %collective-permute-start.1 = (f32[8,2,2,3,3,128]{5,2,4,3,1,0:T(2,128)S(1)}, f32[8,2,2,3,3,128]{5,2,4,3,1,0:T(2,128)S(1)}, u32[]{:S(2)}, u32[]{:S(2)}) collective-permute-start(f32[8,2,2,3,3,128]{5,2,4,3,1,0:T(2,128)S(1)} %get-tuple-element.455), channel_id=1, source_target_pairs={{4,0},{8,4},{12,8},{16,12},{20,16},{24,20},{28,24},{0,28},{5,1},{9... | collective-permute-start | bytes 442376 | tf_op jit(solution)/shard_map/while/body/eval_jaxpr/ppermute | solution.py:12
  23.8 5.2 %collective-permute-start = (f32[2,2,3,3,128]{4,1,3,2,0:T(2,128)S(1)}, f32[2,2,3,3,128]{4,1,3,2,0:T(2,128)S(1)}, u32[]{:S(2)}, u32[]{:S(2)}) collective-permute-start(f32[2,2,3,3,128]{4,1,3,2,0:T(2,128)S(1)} %get-tuple-element.454), channel_id=1, source_target_pairs={{4,0},{8,4},{12,8},{16,12},{20,16},{24,20},{28,24},{0,28},{5,1},{9... | collective-permute-start | bytes 55304 | tf_op jit(solution)/shard_map/while/body/eval_jaxpr/ppermute | solution.py:12
  27.6 2.9 %collective-permute-start.1 = (f32[8,2,2,3,3,128]{5,2,4,3,1,0:T(2,128)S(1)}, f32[8,2,2,3,3,128]{5,2,4,3,1,0:T(2,128)S(1)}, u32[]{:S(2)}, u32[]{:S(2)}) collective-permute-start(f32[8,2,2,3,3,128]{5,2,4,3,1,0:T(2,128)S(1)} %get-tuple-element.455), channel_id=1, source_target_pairs={{4,0},{8,4},{12,8},{16,12},{20,16},{24,20},{28,24},{0,28},{5,1},{9... | collective-permute-start | bytes 442376 | tf_op jit(solution)/shard_map/while/body/eval_jaxpr/ppermute | solution.py:12
  30.7 26.4 %copy-start.3 = (f32[8,8,8,8]{3,2,1,0:T(8,128)S(1)}, f32[8,8,8,8]{3,2,1,0:T(8,128)}, u32[]{:S(2)}) copy-start(f32[8,8,8,8]{3,2,1,0:T(8,128)} %param.13) | copy-start | bytes 49156
  58.4 0.9 copy-start.4
  97.0 1.1 copy-start
  97.7 46.9 %collective-permute-start.2 = (f32[8,2,2,3,3,128]{5,0,4,3,2,1:T(8,128)}, f32[8,2,2,3,3,128]{5,0,4,3,2,1:T(8,128)S(1)}, u32[]{:S(2)}, u32[]{:S(2)}) collective-permute-start(f32[8,2,2,3,3,128]{5,0,4,3,2,1:T(8,128)} %slice.117), channel_id=1, source_target_pairs={{16,0},{20,4},{24,8},{28,12},{0,16},{4,20},{8,24},{12,28},{17,1},{... | collective-permute-start | bytes 442376 | tf_op jit(solution)/shard_map/ppermute | solution.py:12
  97.7 47.0 %collective-permute-start.3 = (f32[8,4,2,3,3,128]{5,0,4,3,2,1:T(8,128)S(1)}, f32[8,4,2,3,3,128]{5,0,4,3,2,1:T(8,128)}, u32[]{:S(2)}, u32[]{:S(2)}) collective-permute-start(f32[8,4,2,3,3,128]{5,0,4,3,2,1:T(8,128)S(1)} %slice.120), channel_id=1, source_target_pairs={{24,0},{28,4},{0,8},{4,12},{8,16},{12,20},{16,24},{20,28},{25,1},{... | collective-permute-start | bytes 884744 | tf_op jit(solution)/shard_map/ppermute | solution.py:12
  102.5 44.1 %copy-start.1 = (f32[8,8,2,1,3,3,128]{6,1,5,4,2,0,3:T(8,128)S(1)}, f32[8,8,2,1,3,3,128]{6,1,5,4,2,0,3:T(8,128)}, u32[]{:S(2)}) copy-start(f32[8,8,2,1,3,3,128]{6,1,5,4,2,0,3:T(8,128)} %get-tuple-element.248) | copy-start | bytes 1769476
  102.5 44.1 %copy-start.2 = (f32[8,8,2,1,3,3,128]{6,1,5,4,2,0,3:T(8,128)S(1)}, f32[8,8,2,1,3,3,128]{6,1,5,4,2,0,3:T(8,128)}, u32[]{:S(2)}) copy-start(f32[8,8,2,1,3,3,128]{6,1,5,4,2,0,3:T(8,128)} %get-tuple-element.249) | copy-start | bytes 1769476
  145.7 6.4 %collective-permute-start.4 = (f32[8,2,2,3,3,128]{5,0,4,3,2,1:T(8,128)S(1)}, f32[8,2,2,3,3,128]{5,0,4,3,2,1:T(8,128)S(1)}, u32[]{:S(2)}, u32[]{:S(2)}) collective-permute-start(f32[8,2,2,3,3,128]{5,0,4,3,2,1:T(8,128)S(1)} %slice.146), channel_id=1, source_target_pairs={{28,0},{0,4},{4,8},{8,12},{12,16},{16,20},{20,24},{24,28},{29,1},{... | collective-permute-start | bytes 442376 | tf_op jit(solution)/shard_map/ppermute | solution.py:12
where the time goes:
time: 154 us; the launch traced here: 153 us
  blocking collectives  42.1 us (27%)
  loops' own time  34.6 us (22%)
  local copies, waits for them, and re-layouts  24.8 us (16%)
  starting transfers between devices  16.8 us (11%)
  waiting for transfers between devices  16.4 us (11%)
  other arithmetic  12.2 us (8%)
  matrix products  5.08 us (3%)
    psum x1, blocking collectives, per_device(): summed = lax.psum(partial_grad, ('gx', 'yz'))  42.1 us
    another operation x1, loops' own time, per_device(): lax.scan(forward_step, gauge_links, offsets)  17.8 us
    ppermute x11, starting transfers between devices, from_behind(): return lax.ppermute(block, axis, route)  16.8 us
    another operation x1, loops' own time, per_device(): lax.scan(backward_step, accumulator, (offsets, line_grad, all_lines))  16.6 us
    ppermute x11, waiting for transfers between devices, from_behind(): return lax.ppermute(block, axis, route)  16.4 us
    dynamic_slice x16, local copies, waits for them, and re-layouts, per_device(): lax.scan(forward_step, gauge_links, offsets)  10 us
    squeeze x8, local copies, waits for them, and re-layouts, per_device(): lax.scan(backward_step, accumulator, (offsets, line_grad, all_lines))  7.41 us
    reduce_sum x41, other arithmetic, matmul_three(): jnp.sum(left[..., :, :, None, :] * right[..., None, :, :, :], axis=-3)  6.43 us
  transfers between devices with their start and end apart: 11, of which 9 were waited for; matrix products, arithmetic and copies ran while one was open for 4% of the time, Pallas kernels for 0%

commit v1 on v0

--- a/solution.py
+++ b/solution.py
@@ -1,9 +1,16 @@
+import functools
 import math
 
 import jax
 import jax.numpy as jnp
 from jax import lax
+from jax.experimental import pallas as pl
+from jax.experimental.pallas import tpu as pltpu
 from jax.sharding import PartitionSpec as P
+
+MESH = pl.DeviceIdType.MESH
+LANES = 128
+VMEM_BYTES = 56 * 1024 * 1024
 
 
 def from_behind(block, axis, distance):
@@ -31,7 +38,7 @@
     return jnp.stack([swapped[..., 0, :, :, :], -swapped[..., 1, :, :, :]], axis=-4)
 
 
-def per_device(gauge_links, in_field, cotangent, bilinear_weights):
+def general(gauge_links, in_field, cotangent, bilinear_weights):
     part_x = gauge_links.shape[0]
     channels = in_field.shape[0]
     line_count = bilinear_weights.shape[2]
@@ -106,6 +113,481 @@
     return (grad_field, grad_weights)
 
 
+def block_transpose(arrays):
+    arrays = list(arrays)
+    lane = lax.broadcasted_iota(jnp.int32, arrays[0].shape, 1)
+    for bit in (1, 2, 4):
+        upper = (lane & (16 * bit)) != 0
+        for r in range(8):
+            if r & bit:
+                continue
+            low, high = arrays[r], arrays[r | bit]
+            arrays[r] = jnp.where(upper, pltpu.roll(high, 16 * bit, 1), low)
+            arrays[r | bit] = jnp.where(upper, high, pltpu.roll(low, LANES - 16 * bit, 1))
+    return arrays
+
+
+def greet(axes):
+    barrier = pltpu.get_barrier_semaphore()
+    total = 0
+    for axis, count in axes:
+        me = lax.axis_index(axis)
+        for k in range(1, count):
+            peer = lax.rem(me + k, count)
+            pl.semaphore_signal(barrier, inc=1, device_id={axis: peer}, device_id_type=MESH)
+        total += count - 1
+    return lambda: pl.semaphore_wait(barrier, total)
+
+
+def exchange(axis, count, source, target, send_sem, recv_sem):
+    me = lax.axis_index(axis)
+
+    def copy(k):
+        peer = lax.rem(me + k, count)
+        return pltpu.make_async_remote_copy(
+            src_ref=source.at[peer],
+            dst_ref=target.at[me],
+            send_sem=send_sem.at[k],
+            recv_sem=recv_sem.at[k],
+            device_id={axis: peer},
+            device_id_type=MESH,
+        )
+
+    def arrival(k):
+        origin = lax.rem(me + count - k, count)
+        return pltpu.make_async_remote_copy(
+            src_ref=source.at[origin],
+            dst_ref=target.at[origin],
+            send_sem=send_sem.at[k],
+            recv_sem=recv_sem.at[k],
+            device_id={axis: origin},
+            device_id_type=MESH,
+        )
+
+    return [copy(k) for k in range(1, count)], [arrival(k) for k in range(1, count)]
+
+
+def gather_kernel(u_ref, w_ref, g_ref, out_ref, packed, sending, landed, send_sem, recv_sem):
+    me = lax.axis_index("gx")
+    ready = greet((("gx", 8),))
+    packed[:, 72:80, :] = jnp.zeros((8, 8, LANES), jnp.float32)
+    for x in range(2):
+        for part in range(2):
+            for a in range(3):
+                row = ((x * 2 + part) * 3 + a) * 3
+                packed[:, row : row + 3, :] = w_ref[:, x, part, a, :, :]
+                packed[:, 36 + row : 39 + row, :] = g_ref[:, x, part, a, :, :]
+                for b in range(3):
+                    r, t = divmod(row + b, 5)
+                    packed[r, 72 + t : 73 + t, :] = u_ref[x, part, a, b : b + 1, :]
+    for start in (0, 40):
+        rows = slice(start, start + 40)
+        for d, value in enumerate(block_transpose([packed[r, rows, :] for r in range(8)])):
+            sending[d, rows, :] = value
+    ready()
+    copies, arrivals = exchange("gx", 8, sending, landed, send_sem, recv_sem)
+    for copy in copies:
+        copy.start()
+    landed[me] = sending[me]
+    for arrival in arrivals:
+        arrival.wait_recv()
+    for start in (0, 40):
+        rows = slice(start, start + 40)
+        for d, value in enumerate(block_transpose([landed[r, rows, :] for r in range(8)])):
+            out_ref[d, rows, :] = value
+    for copy in copies:
+        copy.wait_send()
+
+
+def mm(left, right, left_h=False, right_h=False):
+    def pick(m, h, a, b):
+        return (m[0][b][a], m[1][b][a]) if h else (m[0][a][b], m[1][a][b])
+
+    real = [[None] * 3 for _ in range(3)]
+    imag = [[None] * 3 for _ in range(3)]
+    for a in range(3):
+        for b in range(3):
+            re = im = None
+            for k in range(3):
+                lr, li = pick(left, left_h, a, k)
+                rr, ri = pick(right, right_h, k, b)
+                rr_lr, ii = lr * rr, li * ri
+                re = rr_lr if re is None else re + rr_lr
+                re = re + ii if left_h != right_h else re - ii
+                first, second = lr * ri, li * rr
+                if right_h and left_h:
+                    term = -(first + second)
+                elif right_h:
+                    term = second - first
+                elif left_h:
+                    term = first - second
+                else:
+                    term = first + second
+                im = term if im is None else im + term
+            real[a][b], imag[a][b] = re, im
+    return [real, imag]
+
+
+def map_matrix(f, *ms):
+    return [[[f(*(m[r][a][b] for m in ms)) for b in range(3)] for a in range(3)] for r in range(2)]
+
+
+def comp(r, a, b):
+    return (r * 3 + a) * 3 + b
+
+
+def read_matrix(f):
+    return [[[f(comp(r, a, b)) for b in range(3)] for a in range(3)] for r in range(2)]
+
+
+def each(m):
+    for r in range(2):
+        for a in range(3):
+            for b in range(3):
+                yield comp(r, a, b), m[r][a][b]
+
+
+def conjugate_by(v, m):
+    return mm(mm(v, m), v, right_h=True)
+
+
+def conjugate_by_h(v, m):
+    return mm(mm(v, m, left_h=True), v)
+
+
+def split(value):
+    high = value.astype(jnp.bfloat16)
+    return high, (value - high.astype(jnp.float32)).astype(jnp.bfloat16)
+
+
+def compute_kernel(
+    b_ref, w3_ref, wt3_ref, back_ref, gw_ref, field, cot, wrapped, v_all, v_wrap, z, pair, mixed, line, total, final
+):
+    lane1 = lax.broadcasted_iota(jnp.int32, (1, LANES), 1)
+    lane = lax.broadcasted_iota(jnp.int32, (8, LANES), 1)
+    with jax.named_scope("frames"):
+        def link(p, c):
+            r, t = divmod(p * 18 + c, 5)
+            return b_ref[pl.ds(r * 80 + 72 + t, 1), :]
+
+        u0 = read_matrix(lambda c: link(0, c))
+        u1 = read_matrix(lambda c: link(1, c))
+        one = [[[jnp.float32(1.0 if r == 0 and a == b else 0.0) for b in range(3)] for a in range(3)] for r in range(2)]
+        prefix = mm(u0, u1)
+        for step in (1, 2, 4):
+            before = map_matrix(
+                lambda m, i: jnp.where(lane1 >= 16 * step, pltpu.roll(m, 16 * step, 1), i), prefix, one
+            )
+            prefix = mm(before, prefix)
+        start = map_matrix(lambda m, i: jnp.where(lane1 >= 16, pltpu.roll(m, 16, 1), i), prefix, one)
+
+        def last_group(m):
+            m = jnp.where(lane1 >= 112, m, 0.0)
+            for step in (1, 2, 4):
+                m = m + pltpu.roll(m, 16 * step, 1)
+            return m
+
+        loop = map_matrix(last_group, prefix)
+        odd = mm(start, u0)
+        for p, m in enumerate((start, odd)):
+            for c, value in each(m):
+                v_all[c, p] = jnp.broadcast_to(value, (8, LANES))
+            for c, value in each(mm(loop, m)):
+                v_wrap[c, p] = jnp.broadcast_to(value, (8, LANES))
+
+    with jax.named_scope("to_frame"):
+        for p in range(2):
+            v = read_matrix(lambda c: v_all[c, p])
+            vw = read_matrix(lambda c: v_wrap[c, p])
+            w = read_matrix(lambda c: b_ref[pl.ds(p * 18 + c, 8, stride=80), :])
+            g = read_matrix(lambda c: b_ref[pl.ds(36 + p * 18 + c, 8, stride=80), :])
+            for c, value in each(conjugate_by(v, w)):
+                field[c, p] = value
+            for c, value in each(conjugate_by(vw, w)):
+                wrapped[c, p] = value
+            for c, value in each(conjugate_by(v, g)):
+                cot[c, p] = value
+
+    with jax.named_scope("window"):
+        for c in range(18):
+            pieces = []
+            for t in range(9):
+                q, k = (t + 1) % 2, (t + 1) // 2
+                if k == 0:
+                    pieces.append(field[c, q])
+                else:
+                    joined = jnp.where(lane < 16 * k, wrapped[c, q], field[c, q])
+                    pieces.append(pltpu.roll(joined, LANES - 16 * k, 1))
+            pieces.append(jnp.zeros((8, LANES), jnp.float32))
+            high, low = split(jnp.concatenate(pieces, axis=0))
+            columns = slice(c * LANES, (c + 1) * LANES)
+            z[0:80, columns] = high
+            z[80:160, columns] = low
+            z[160:240, columns] = high
+
+    with jax.named_scope("pairs"):
+        @pl.loop(0, 8)
+        def _(i):
+            for p in range(2):
+                w = read_matrix(lambda c: field[c, p])
+                g = read_matrix(lambda c: jnp.broadcast_to(cot[c, p, pl.ds(i, 1), :], (8, LANES)))
+                row = pl.multiple_of(p * 64 + i * 8, 8)
+                for c, value in each(mm(w, g, left_h=True)):
+                    pair[pl.ds(row, 8), c * LANES : (c + 1) * LANES] = value
+
+    with jax.named_scope("products"):
+        def rows_of(ref, width, edge):
+            value = ref[...]
+            at = lax.broadcasted_iota(jnp.int32, value.shape, 1)
+            high = value.astype(jnp.bfloat16).astype(jnp.float32)
+            return jnp.where(at < edge, high, value - high).astype(jnp.bfloat16)
+
+        w3 = rows_of(w3_ref, 240, 160)
+        wt3 = rows_of(wt3_ref, 384, 256)
+        weights = jnp.zeros((256, 160), jnp.float32)
+        for chunk in range(9):
+            columns = slice(chunk * 256, (chunk + 1) * 256)
+            high, low = split(pair[:, columns])
+            zc = z[:, columns]
+            weights = weights + lax.dot_general(
+                jnp.concatenate([high, low], axis=0),
+                zc[0:160],
+                (((1,), (1,)), ((), ())),
+                preferred_element_type=jnp.float32,
+            )
+            mixed[:, columns] = jnp.dot(w3, zc, preferred_element_type=jnp.float32)
+            line[:, columns] = jnp.dot(
+                wt3, jnp.concatenate([high, low, high], axis=0), preferred_element_type=jnp.float32
+            )
+        half = weights[0:128] + weights[128:256]
+        both = half[:, 0:80] + half[:, 80:160]
+        gw_ref[...] = jnp.zeros((64, LANES), jnp.float32)
+        gw_ref[:, 0:64] = both[0:64, 0:64] + both[64:128, 8:72]
+
+    with jax.named_scope("direct"):
+        for p in range(2):
+            @pl.loop(0, 3)
+            def _(a):
+                sums = [[None, None] for _ in range(3)]
+                for i in range(8):
+                    rows = slice(p * 64 + i * 8, p * 64 + i * 8 + 8)
+                    for k in range(3):
+                        gr = jnp.broadcast_to(cot[a * 3 + k, p, i : i + 1, :], (8, LANES))
+                        gi = jnp.broadcast_to(cot[9 + a * 3 + k, p, i : i + 1, :], (8, LANES))
+                        for b in range(3):
+                            at = comp(0, b, k) * LANES
+                            mr = mixed[rows, at : at + LANES]
+                            at = comp(1, b, k) * LANES
+                            mi = mixed[rows, at : at + LANES]
+                            re = gr * mr + gi * mi
+                            im = gi * mr - gr * mi
+                            s = sums[b]
+                            sums[b] = [re, im] if s[0] is None else [s[0] + re, s[1] + im]
+                for b in range(3):
+                    total[a * 3 + b, p] = sums[b][0]
+                    total[9 + a * 3 + b, p] = sums[b][1]
+
+    with jax.named_scope("from_frame"):
+        final[...] = jnp.zeros((320, LANES), jnp.float32)
+        for q in range(2):
+            near, far = {}, {}
+            for c in range(18):
+                inside, outside = total[c, q], None
+                for t in range(9):
+                    if (t + 1) % 2 != q:
+                        continue
+                    k = (t + 1) // 2
+                    piece = line[t * 8 : t * 8 + 8, c * LANES : (c + 1) * LANES]
+                    if k == 0:
+                        inside = inside + piece
+                        continue
+                    piece = pltpu.roll(piece, 16 * k, 1)
+                    inside = inside + jnp.where(lane >= 16 * k, piece, 0.0)
+                    beyond = jnp.where(lane < 16 * k, piece, 0.0)
+                    outside = beyond if outside is None else outside + beyond
+                near[c], far[c] = inside, outside
+            first = conjugate_by_h(read_matrix(lambda c: v_all[c, q]), read_matrix(lambda c: near[c]))
+            second = conjugate_by_h(read_matrix(lambda c: v_wrap[c, q]), read_matrix(lambda c: far[c]))
+            for c, value in each(map_matrix(lambda m, n: m + n, first, second)):
+                final[pl.ds(q * 18 + c, 8, stride=40), :] = value
+        for d, value in enumerate(block_transpose([final[r * 40 : r * 40 + 40, :] for r in range(8)])):
+            back_ref[d] = value
+
+
+def return_kernel(
+    scale,
+    yz_count,
+    back_ref,
+    gw_ref,
+    out_ref,
+    gw_out,
+    landed,
+    shares,
+    across,
+    mine,
+    whole,
+    send_sem,
+    recv_sem,
+    share_send,
+    share_recv,
+    across_send,
+    across_recv,
+    whole_send,
+    whole_recv,
+):
+    me = lax.axis_index("gx")
+    here = lax.axis_index("yz")
+    greet((("gx", 8), ("yz", yz_count)))()
+    share_copies, share_arrivals = exchange("gx", 8, gw_ref, shares, share_send, share_recv)
+    copies, arrivals = exchange("gx", 8, back_ref, landed, send_sem, recv_sem)
+    for copy in share_copies:
+        copy.start()
+    for copy in copies:
+        copy.start()
+    landed[me] = back_ref[me]
+    shares[me] = gw_ref[me]
+    for arrival in share_arrivals:
+        arrival.wait_recv()
+    subtotal = shares[0]
+    for s in range(1, 8):
+        subtotal = subtotal + shares[s]
+    mine[...] = subtotal
+
+    def spread(axis, count, source, target, send, recv):
+        at = lax.axis_index(axis)
+        outgoing, incoming = [], []
+        for k in range(1, count):
+            for found, slot, there in (
+                (outgoing, at, lax.rem(at + k, count)),
+                (incoming, lax.rem(at + count - k, count), lax.rem(at + count - k, count)),
+            ):
+                found.append(
+                    pltpu.make_async_remote_copy(
+                        src_ref=source,
+                        dst_ref=target.at[slot],
+                        send_sem=send.at[k],
+                        recv_sem=recv.at[k],
+                        device_id={axis: there},
+                        device_id_type=MESH,
+                    )
+                )
+        return outgoing, incoming
+
+    across_copies, across_arrivals = spread("yz", yz_count, mine, across, across_send, across_recv)
+    for copy in across_copies:
+        copy.start()
+    across[here] = subtotal
+    for arrival in across_arrivals:
+        arrival.wait_recv()
+    summed = across[0]
+    for s in range(1, yz_count):
+        summed = summed + across[s]
+    summed = summed * scale
+    whole[me] = summed
+    whole_copies, whole_arrivals = spread("gx", 8, whole.at[me], whole, whole_send, whole_recv)
+    for copy in whole_copies:
+        copy.start()
+    for arrival in arrivals:
+        arrival.wait_recv()
+    rows = block_transpose([landed[r] for r in range(8)])
+    for c in range(8):
+        for x in range(2):
+            for part in range(2):
+                for a in range(3):
+                    row = ((x * 2 + part) * 3 + a) * 3
+                    out_ref[c, x, part, a, :, :] = rows[c][row : row + 3]
+    for arrival in whole_arrivals:
+        arrival.wait_recv()
+    gw_out[...] = whole[...]
+    for copy in share_copies + copies + across_copies + whole_copies:
+        copy.wait_send()
+
+
+def resident(scale, yz_count, gauge_links, in_field, cotangent, bilinear_weights):
+    f32 = jnp.float32
+    vmem = pl.BlockSpec(memory_space=pltpu.VMEM)
+    dma = pltpu.SemaphoreType.DMA
+    gathered = pl.pallas_call(
+        gather_kernel,
+        out_shape=jax.ShapeDtypeStruct((8, 80, LANES), f32),
+        in_specs=[vmem] * 3,
+        out_specs=vmem,
+        scratch_shapes=[pltpu.VMEM((8, 80, LANES), f32)] * 3 + [dma((8,)), dma((8,))],
+        compiler_params=pltpu.CompilerParams(
+            collective_id=0, has_side_effects=True, vmem_limit_bytes=VMEM_BYTES
+        ),
+        name="gather_sites",
+    )(gauge_links, in_field, cotangent)
+    rows = bilinear_weights.reshape(64, 64)
+    shifted = jnp.concatenate(
+        [jnp.pad(rows, ((0, 0), (0, 16))), jnp.pad(rows, ((0, 0), (8, 8)))], axis=0
+    )
+    w3 = jnp.concatenate([shifted] * 3, axis=1)
+    wt3 = jnp.concatenate([shifted.T] * 3, axis=1)
+    back, partial = pl.pallas_call(
+        compute_kernel,
+        out_shape=(
+            jax.ShapeDtypeStruct((8, 40, LANES), f32),
+            jax.ShapeDtypeStruct((64, LANES), f32),
+        ),
+        in_specs=[vmem] * 3,
+        out_specs=(vmem, vmem),
+        scratch_shapes=[
+            pltpu.VMEM((18, 2, 8, LANES), f32),
+            pltpu.VMEM((18, 2, 8, LANES), f32),
+            pltpu.VMEM((18, 2, 8, LANES), f32),
+            pltpu.VMEM((18, 2, 8, LANES), f32),
+            pltpu.VMEM((18, 2, 8, LANES), f32),
+            pltpu.VMEM((240, 18 * LANES), jnp.bfloat16),
+            pltpu.VMEM((128, 18 * LANES), f32),
+            pltpu.VMEM((128, 18 * LANES), f32),
+            pltpu.VMEM((80, 18 * LANES), f32),
+            pltpu.VMEM((18, 2, 8, LANES), f32),
+            pltpu.VMEM((320, LANES), f32),
+        ],
+        compiler_params=pltpu.CompilerParams(vmem_limit_bytes=VMEM_BYTES),
+        name="lattice_products",
+    )(gathered.reshape(640, LANES), w3, wt3)
+    grad_field, grad_weights = pl.pallas_call(
+        functools.partial(return_kernel, scale, yz_count),
+        out_shape=(
+            jax.ShapeDtypeStruct((8, 2, 2, 3, 3, LANES), f32),
+            jax.ShapeDtypeStruct((8, 8, LANES), f32),
+        ),
+        in_specs=[vmem] * 2,
+        out_specs=(vmem, vmem),
+        scratch_shapes=[
+            pltpu.VMEM((8, 40, LANES), f32),
+            pltpu.VMEM((8, 8, LANES), f32),
+            pltpu.VMEM((yz_count, 8, LANES), f32),
+            pltpu.VMEM((8, LANES), f32),
+            pltpu.VMEM((8, 8, LANES), f32),
+        ]
+        + [dma((8,)), dma((8,)), dma((8,)), dma((8,))]
+        + [dma((yz_count,)), dma((yz_count,)), dma((8,)), dma((8,))],
+        compiler_params=pltpu.CompilerParams(
+            collective_id=1, has_side_effects=True, vmem_limit_bytes=VMEM_BYTES
+        ),
+        name="return_sites",
+    )(back, partial.reshape(8, 8, LANES))
+    return grad_field, grad_weights[:, :, 0:64].reshape(8, 8, 8, 8)
+
+
+def per_device(gauge_links, in_field, cotangent, bilinear_weights):
+    gx = lax.axis_size("gx")
+    yz = lax.axis_size("yz")
+    fits = (
+        gx == 8
+        and in_field.shape == (8, 2, 2, 3, 3, LANES)
+        and bilinear_weights.shape == (8, 8, 8, 8)
+    )
+    if not fits:
+        return general(gauge_links, in_field, cotangent, bilinear_weights)
+    total = gauge_links.shape[0] * gx * gauge_links.shape[-1] * yz
+    scale = 1.0 / math.sqrt(100.0 * total)
+    return resident(scale, yz, gauge_links, in_field, cotangent, bilinear_weights)
+
+
 def solution(mesh):
     placed = (
         P("gx", None, None, None, "yz"),

time: 154 us -> 46 us (0.30)
  blocking collectives: 42.1 us -> 0 us
  Pallas kernels: 0 us -> 37 us
  loops' own time: 34.6 us -> 0 us
  local copies, waits for them, and re-layouts: 24.8 us -> 7.22 us
  starting transfers between devices: 16.8 us -> 0 us
  waiting for transfers between devices: 16.4 us -> 0 us
  other arithmetic: 12.2 us -> 0.83 us
  matrix products: 5.08 us -> 0 us
    psum x1 -> x0, blocking collectives: 42.1 us -> none  [per_device(): summed = lax.psum(partial_grad, ('gx', 'yz'))]
    pallas_call x0 -> x3, Pallas kernels: none -> 37 us  [the longest x1 18.1 us: resident(): pl.pallas_call(functools.partial(return_kernel, scale, yz_count), out_sha...]
    another operation x3 -> x0, loops' own time: 34.6 us -> none  [the longest x1 17.8 us: per_device(): lax.scan(forward_step, gauge_links, offsets)]
    ppermute x11 -> x0, starting transfers between devices: 16.8 us -> none  [from_behind(): return lax.ppermute(block, axis, route)]
    ppermute x11 -> x0, waiting for transfers between devices: 16.4 us -> none  [from_behind(): return lax.ppermute(block, axis, route)]
    dynamic_slice x24 -> x0, local copies, waits for them, and re-layouts: 10.2 us -> none  [the longest x16 10 us: per_device(): lax.scan(forward_step, gauge_links, offsets)]
    squeeze x8 -> x0, local copies, waits for them, and re-layouts: 7.41 us -> none  [per_device(): lax.scan(backward_step, accumulator, (offsets, line_grad, all_lines))]
    reduce_sum x42 -> x0, other arithmetic: 6.48 us -> none  [the longest x41 6.43 us: matmul_three(): jnp.sum(left[..., :, :, None, :] * right[..., None, :, :, :], axis=-3)]
  transfers between devices with their start and end apart: 11 -> 0, of which waited for: 9 -> 0; matrix products, arithmetic and copies ran while one was open for 4% -> 0% of each run, Pallas kernels for 0% -> 0%
where the time goes in v1:
time: 46 us; the launch traced here: 45.7 us
  Pallas kernels  37 us (80%)
  local copies, waits for them, and re-layouts  7.22 us (16%)
  other arithmetic  0.83 us (2%)
  between operations  0.69 us (2%)
    pallas_call x1, Pallas kernels, resident(): pl.pallas_call(functools.partial(return_kernel, scale, yz_count), out_sha...  18.1 us
    pallas_call x1, Pallas kernels, resident(): pl.pallas_call(gather_kernel, out_shape=jax.ShapeDtypeStruct((8, 80, LANE...  13.4 us
    pallas_call x1, Pallas kernels, resident(): pl.pallas_call(compute_kernel, out_shape=(jax.ShapeDtypeStruct((8, 40, LA...  5.5 us
    unnamed x10, local copies, waits for them, and re-layouts  5.42 us

profile of v1, /device:TPU:0, one launch (start us, length us, event | category | flops | bytes accessed | tf_op | source)
XLA Modules:
  0.0 45.7 jit_solution(2734722897772891559)
XLA Ops:
  0.6 1.3 %copy.6.u_ref = f32[2,2,3,3,128]{4,3,2,1,0:T(4,128)} copy(f32[2,2,3,3,128]{4,1,3,2,0:T(2,128)} %param.4) | data formatting | bytes 36864 | tf_op args[0]
  2.0 0.0 copy-start.1
  2.0 1.7 %copy.7.w_ref = f32[8,2,2,3,3,128]{5,4,3,2,1,0:T(4,128)} copy(f32[8,2,2,3,3,128]{5,2,4,3,1,0:T(2,128)} %param.5) | data formatting | bytes 294912 | tf_op args[1]
  3.6 0.0 copy-done.1
  3.6 0.7 %copy.8.g_ref = f32[8,2,2,3,3,128]{5,4,3,2,1,0:T(4,128)} copy(f32[8,2,2,3,3,128]{5,2,4,3,1,0:T(2,128)S(1)} %copy-done.1) | data formatting | bytes 294912 | tf_op args[2]
  4.4 0.0 copy-start
  4.4 13.4 %gather_sites.1 = f32[8,80,128]{2,1,0:T(8,128)} custom-call(f32[2,2,3,3,128]{4,3,2,1,0:T(4,128)} %copy.6.u_ref, f32[8,2,2,3,3,128]{5,4,3,2,1,0:T(4,128)} %copy.7.w_ref, f32[8,2,2,3,3,128]{5,4,3,2,1,0:T(4,128)} %copy.8.g_ref), custom_call_target="tpu_custom_call" | custom-call | tf_op jit(solution)/shard_map/gather_sites/pallas_call | solution.py:510
  17.7 0.0 copy-done
  17.8 0.1 reshape.20
  17.9 0.1 copy.12
  18.0 0.1 maximum_maximum_fusion
  18.1 0.8 %copy.10.w3_ref = f32[128,240]{1,0:T(8,128)} copy(f32[128,240]{0,1:T(8,128)S(1)} %maximum_maximum_fusion) | data formatting | bytes 245760 | tf_op jit(solution)/shard_map/concatenate | solution.py:525
  18.8 0.1 maximum_bitcast_fusion
  18.9 0.6 %pad_maximum_fusion.wt3_ref = f32[80,384]{1,0:T(8,128)} fusion(f32[80,128]{1,0:T(8,128)S(1)} %maximum_bitcast_fusion), kind=kLoop, calls=%fused_computation.1 | loop fusion | flops 61440 | bytes 163840 | tf_op jit(solution)/shard_map/concatenate | solution.py:526
  19.6 5.5 %lattice_products.1 = (f32[8,40,128]{2,1,0:T(8,128)}, f32[64,128]{1,0:T(8,128)}) custom-call(f32[640,128]{1,0:T(8,128)} %bitcast.7, f32[128,240]{1,0:T(8,128)} %copy.10.w3_ref, f32[80,384]{1,0:T(8,128)} %pad_maximum_fusion.wt3_ref), custom_call_target="tpu_custom_call" | custom-call | tf_op jit(solution)/shard_map/lattice_products/pallas_call | solution.py:527
  25.1 18.1 %return_sites.1 = (f32[8,2,2,3,3,128]{5,4,3,2,1,0:T(4,128)}, f32[8,8,128]{2,1,0:T(8,128)}) custom-call(f32[8,40,128]{2,1,0:T(8,128)} %get-tuple-element.6.back_ref, f32[8,8,128]{2,1,0:T(8,128)} %bitcast.9), custom_call_target="tpu_custom_call" | custom-call | tf_op jit(solution)/shard_map/return_sites/pallas_call | solution.py:551
  43.2 0.0 copy-start.2
  43.2 1.7 %copy.11 = f32[8,2,2,3,3,128]{5,2,4,3,1,0:T(2,128)} copy(f32[8,2,2,3,3,128]{5,4,3,2,1,0:T(4,128)} %get-tuple-element.10) | data formatting | bytes 294912
  44.9 0.0 copy-done.2
  44.9 0.8 %reshape.19 = f32[8,8,8,8]{3,2,1,0:T(8,128)} reshape(f32[8,8,64]{2,1,0:T(8,128)S(1)} %bitcast.8) | data formatting | bytes 32768 | tf_op jit(solution)/shard_map/reshape | solution.py:573
  (1 shorter events, 0.0 us)
Async XLA Ops:
  2.0 1.7 %copy-start.1 = (f32[8,2,2,3,3,128]{5,2,4,3,1,0:T(2,128)S(1)}, f32[8,2,2,3,3,128]{5,2,4,3,1,0:T(2,128)}, u32[]{:S(2)}) copy-start(f32[8,2,2,3,3,128]{5,2,4,3,1,0:T(2,128)} %param.6) | copy-start | bytes 442372
  4.4 13.4 %copy-start = (f32[8,8,8,8]{3,2,1,0:T(8,128)S(1)}, f32[8,8,8,8]{3,2,1,0:T(8,128)}, u32[]{:S(2)}) copy-start(f32[8,8,8,8]{3,2,1,0:T(8,128)} %param.7) | copy-start | bytes 49156
  43.2 1.7 %copy-start.2 = (f32[8,8,128]{2,1,0:T(8,128)S(1)}, f32[8,8,128]{2,1,0:T(8,128)}, u32[]{:S(2)}) copy-start(f32[8,8,128]{2,1,0:T(8,128)} %get-tuple-element.9) | copy-start | bytes 98308

commit v2 on v0

--- a/solution.py
+++ b/solution.py
@@ -1,9 +1,16 @@
+import functools
 import math
 
 import jax
 import jax.numpy as jnp
 from jax import lax
+from jax.experimental import pallas as pl
+from jax.experimental.pallas import tpu as pltpu
 from jax.sharding import PartitionSpec as P
+
+MESH = pl.DeviceIdType.MESH
+LANES = 128
+VMEM_BYTES = 56 * 1024 * 1024
 
 
 def from_behind(block, axis, distance):
@@ -31,7 +38,7 @@
     return jnp.stack([swapped[..., 0, :, :, :], -swapped[..., 1, :, :, :]], axis=-4)
 
 
-def per_device(gauge_links, in_field, cotangent, bilinear_weights):
+def general(gauge_links, in_field, cotangent, bilinear_weights):
     part_x = gauge_links.shape[0]
     channels = in_field.shape[0]
     line_count = bilinear_weights.shape[2]
@@ -106,6 +113,509 @@
     return (grad_field, grad_weights)
 
 
+def block_transpose(arrays):
+    arrays = list(arrays)
+    lane = lax.broadcasted_iota(jnp.int32, arrays[0].shape, 1)
+    for bit in (1, 2, 4):
+        upper = (lane & (16 * bit)) != 0
+        for r in range(8):
+            if r & bit:
+                continue
+            low, high = arrays[r], arrays[r | bit]
+            arrays[r] = jnp.where(upper, pltpu.roll(high, 16 * bit, 1), low)
+            arrays[r | bit] = jnp.where(upper, high, pltpu.roll(low, LANES - 16 * bit, 1))
+    return arrays
+
+
+def greet(axes):
+    barrier = pltpu.get_barrier_semaphore()
+    total = 0
+    for axis, count in axes:
+        me = lax.axis_index(axis)
+        for k in range(1, count):
+            peer = lax.rem(me + k, count)
+            pl.semaphore_signal(barrier, inc=1, device_id={axis: peer}, device_id_type=MESH)
+        total += count - 1
+    return lambda: pl.semaphore_wait(barrier, total)
+
+
+def spread(axis, count, source, target, send, recv):
+    at = lax.axis_index(axis)
+    outgoing, incoming = [], []
+    for k in range(1, count):
+        for found, slot, there in (
+            (outgoing, at, lax.rem(at + k, count)),
+            (incoming, lax.rem(at + count - k, count), lax.rem(at + count - k, count)),
+        ):
+            found.append(
+                pltpu.make_async_remote_copy(
+                    src_ref=source,
+                    dst_ref=target.at[slot],
+                    send_sem=send.at[k],
+                    recv_sem=recv.at[k],
+                    device_id={axis: there},
+                    device_id_type=MESH,
+                )
+            )
+    return outgoing, incoming
+
+
+def exchange(source, target, rows, send_sem, recv_sem):
+    me = lax.axis_index("gx")
+    outgoing, incoming = [], []
+    for k in range(1, 8):
+        for found, here, slot, there in (
+            (outgoing, lax.rem(me + k, 8), me, lax.rem(me + k, 8)),
+            (incoming, lax.rem(me + k, 8), lax.rem(me + 8 - k, 8), lax.rem(me + 8 - k, 8)),
+        ):
+            found.append(
+                pltpu.make_async_remote_copy(
+                    src_ref=source.at[here, rows, :],
+                    dst_ref=target.at[slot, rows, :],
+                    send_sem=send_sem.at[k],
+                    recv_sem=recv_sem.at[k],
+                    device_id={"gx": there},
+                    device_id_type=MESH,
+                )
+            )
+    return outgoing, incoming
+
+
+def whole_kernel(
+    scale,
+    yz_count,
+    u_ref,
+    w_ref,
+    g_ref,
+    weight_ref,
+    out_ref,
+    gw_out,
+    packed,
+    sending,
+    landed,
+    sites,
+    field,
+    cot,
+    wrapped,
+    v_all,
+    v_wrap,
+    rows_ref,
+    z,
+    pair,
+    mixed,
+    line,
+    total,
+    final,
+    back,
+    returned,
+    partial,
+    shares,
+    mine,
+    across,
+    whole,
+    first_send,
+    first_recv,
+    second_send,
+    second_recv,
+    back_send,
+    back_recv,
+    share_send,
+    share_recv,
+    across_send,
+    across_recv,
+    whole_send,
+    whole_recv,
+):
+    me = lax.axis_index("gx")
+    here = lax.axis_index("yz")
+    ready = greet((("gx", 8), ("yz", yz_count)))
+    lane1 = lax.broadcasted_iota(jnp.int32, (1, LANES), 1)
+    lane = lax.broadcasted_iota(jnp.int32, (8, LANES), 1)
+    early, late = slice(0, 48), slice(48, 80)
+
+    with jax.named_scope("pack"):
+        packed[:, 32:48, :] = jnp.zeros((8, 16, LANES), jnp.float32)
+        packed[:, 72:80, :] = jnp.zeros((8, 8, LANES), jnp.float32)
+        for x in range(2):
+            for ab in range(9):
+                row = x * 18 + ab * 2
+                packed[:, row : row + 2, :] = w_ref[:, x, ab // 3, ab % 3, :, :]
+                packed[:, 41 + row : 43 + row, :] = g_ref[:, x, ab // 3, ab % 3, :, :]
+                for part in range(2):
+                    r, t = divmod(row + part, 5)
+                    packed[r, 36 + t : 37 + t, :] = u_ref[x, ab // 3, ab % 3, part : part + 1, :]
+        started = []
+        arrivals = []
+        for rows, send, recv in ((early, first_send, first_recv), (late, second_send, second_recv)):
+            for d, value in enumerate(block_transpose([packed[r, rows, :] for r in range(8)])):
+                sending[d, rows, :] = value
+            if not started:
+                ready()
+            copies, incoming = exchange(sending, landed, rows, send, recv)
+            for copy in copies:
+                copy.start()
+            started += copies
+            arrivals.append(incoming)
+        landed[me] = sending[me]
+
+    with jax.named_scope("weights"):
+        rows_ref[...] = jnp.zeros((128, 256), jnp.float32)
+        for i in range(8):
+            pieces = [weight_ref[pl.ds(i * 64 + l, 8, stride=8), :] for l in range(8)]
+            joined = jnp.concatenate(pieces, axis=1)
+            rows_ref[i * 8 : i * 8 + 8, 0:64] = joined
+            rows_ref[64 + i * 8 : 72 + i * 8, 8:72] = joined
+        value = rows_ref[...]
+        high = value.astype(jnp.bfloat16).astype(jnp.float32)
+        low = value - high
+        w3 = (high + pltpu.roll(high, 80, 1) + pltpu.roll(low, 160, 1)).astype(jnp.bfloat16)
+        turned = value[:, 0:LANES].T[0:80]
+        high, low = split(turned)
+        wt3 = jnp.concatenate([high, high, low], axis=1)
+
+    with jax.named_scope("links_and_field"):
+        for arrival in arrivals[0]:
+            arrival.wait_recv()
+        for c, value in enumerate(block_transpose([landed[r, early, :] for r in range(8)])):
+            sites[c * 80 : c * 80 + 48, :] = value
+
+        def link(p, c):
+            r, t = divmod(p * 18 + c, 5)
+            return sites[r * 80 + 36 + t : r * 80 + 37 + t, :]
+
+        u0 = read_matrix(lambda c: link(0, c))
+        u1 = read_matrix(lambda c: link(1, c))
+        one = [[[jnp.float32(1.0 if r == 0 and a == b else 0.0) for b in range(3)] for a in range(3)] for r in range(2)]
+        prefix = mm(u0, u1)
+        for step in (1, 2, 4):
+            before = map_matrix(
+                lambda m, i: jnp.where(lane1 >= 16 * step, pltpu.roll(m, 16 * step, 1), i), prefix, one
+            )
+            prefix = mm(before, prefix)
+        start = map_matrix(lambda m, i: jnp.where(lane1 >= 16, pltpu.roll(m, 16, 1), i), prefix, one)
+
+        def last_group(m):
+            m = jnp.where(lane1 >= 112, m, 0.0)
+            for step in (1, 2, 4):
+                m = m + pltpu.roll(m, 16 * step, 1)
+            return m
+
+        loop = map_matrix(last_group, prefix)
+        odd = mm(start, u0)
+        for p, m in enumerate((start, odd)):
+            for c, value in each(m):
+                v_all[c, p] = jnp.broadcast_to(value, (8, LANES))
+            for c, value in each(mm(loop, m)):
+                v_wrap[c, p] = jnp.broadcast_to(value, (8, LANES))
+
+        def read_sites(base):
+            return read_matrix(
+                lambda c: jnp.stack([sites[pl.ds(base + p * 18 + c, 8, stride=80), :] for p in range(2)])
+            )
+
+        v = read_matrix(lambda c: v_all[c])
+        w = read_sites(0)
+        for c, value in each(conjugate_by(v, w)):
+            field[c] = value
+        for c, value in each(conjugate_by(read_matrix(lambda c: v_wrap[c]), w)):
+            wrapped[c] = value
+
+    with jax.named_scope("window"):
+        z[240:256, :] = jnp.zeros((16, 18 * LANES), jnp.bfloat16)
+        for c in range(18):
+            pieces = []
+            for t in range(9):
+                q, k = (t + 1) % 2, (t + 1) // 2
+                if k == 0:
+                    pieces.append(field[c, q])
+                else:
+                    joined = jnp.where(lane < 16 * k, wrapped[c, q], field[c, q])
+                    pieces.append(pltpu.roll(joined, LANES - 16 * k, 1))
+            pieces.append(jnp.zeros((8, LANES), jnp.float32))
+            high, low = split(jnp.concatenate(pieces, axis=0))
+            columns = slice(c * LANES, (c + 1) * LANES)
+            z[0:80, columns] = high
+            z[80:160, columns] = low
+            z[160:240, columns] = high
+
+    with jax.named_scope("pairs"):
+        for arrival in arrivals[1]:
+            arrival.wait_recv()
+        for c, value in enumerate(block_transpose([landed[r, late, :] for r in range(8)])):
+            sites[c * 80 + 48 : c * 80 + 80, :] = value
+        v = read_matrix(lambda c: v_all[c])
+        for c, value in each(conjugate_by(v, read_sites(41))):
+            cot[c] = value
+
+        @pl.loop(0, 8)
+        def _(i):
+            for p in range(2):
+                w = read_matrix(lambda c: field[c, p])
+                g = read_matrix(lambda c: jnp.broadcast_to(cot[c, p, pl.ds(i, 1), :], (8, LANES)))
+                row = pl.multiple_of(p * 64 + i * 8, 8)
+                for c, value in each(mm(w, g, left_h=True)):
+                    pair[pl.ds(row, 8), c * LANES : (c + 1) * LANES] = value
+
+    with jax.named_scope("products"):
+        weights = jnp.zeros((256, 160), jnp.float32)
+        for chunk in range(9):
+            columns = slice(chunk * 256, (chunk + 1) * 256)
+            high, low = split(pair[:, columns])
+            zc = z[:, columns]
+            weights = weights + lax.dot_general(
+                jnp.concatenate([high, low], axis=0),
+                zc[0:160],
+                (((1,), (1,)), ((), ())),
+                preferred_element_type=jnp.float32,
+            )
+            mixed[:, columns] = jnp.dot(w3, zc, preferred_element_type=jnp.float32)
+            line[:, columns] = jnp.dot(
+                wt3, jnp.concatenate([high, low, high], axis=0), preferred_element_type=jnp.float32
+            )
+        half = weights[0:128] + weights[128:256]
+        both = half[:, 0:80] + half[:, 80:160]
+        both = both[0:64, 0:64] + both[64:128, 8:72]
+        both = jnp.concatenate([both, jnp.zeros((64, 64), jnp.float32)], axis=1)
+        for d in range(8):
+            partial[d] = both[d * 8 : d * 8 + 8]
+        share_copies, share_arrivals = exchange(partial, shares, slice(0, 8), share_send, share_recv)
+        for copy in share_copies:
+            copy.start()
+        shares[me] = partial[me]
+        started += share_copies
+
+    with jax.named_scope("direct"):
+        @pl.loop(0, 3)
+        def _(a):
+            for p in range(2):
+                sums = [[None, None] for _ in range(3)]
+                for i in range(8):
+                    rows = slice(p * 64 + i * 8, p * 64 + i * 8 + 8)
+                    for k in range(3):
+                        at = (a * 3 + k) * 2
+                        gr = jnp.broadcast_to(cot[at, p, i : i + 1, :], (8, LANES))
+                        gi = jnp.broadcast_to(cot[at + 1, p, i : i + 1, :], (8, LANES))
+                        for b in range(3):
+                            at = comp(0, b, k) * LANES
+                            mr = mixed[rows, at : at + LANES]
+                            at = comp(1, b, k) * LANES
+                            mi = mixed[rows, at : at + LANES]
+                            re = gr * mr + gi * mi
+                            im = gi * mr - gr * mi
+                            s = sums[b]
+                            sums[b] = [re, im] if s[0] is None else [s[0] + re, s[1] + im]
+                for b in range(3):
+                    total[(a * 3 + b) * 2, p] = sums[b][0]
+                    total[(a * 3 + b) * 2 + 1, p] = sums[b][1]
+
+    with jax.named_scope("share_sum"):
+        for arrival in share_arrivals:
+            arrival.wait_recv()
+        subtotal = shares[0]
+        for s in range(1, 8):
+            subtotal = subtotal + shares[s]
+        mine[...] = subtotal
+        across_copies, across_arrivals = spread("yz", yz_count, mine, across, across_send, across_recv)
+        for copy in across_copies:
+            copy.start()
+        across[here] = subtotal
+        started += across_copies
+
+    with jax.named_scope("from_frame"):
+        near, far = {}, {}
+        for c in range(18):
+            insides, outsides = [], []
+            for q in range(2):
+                inside, outside = total[c, q], None
+                for t in range(9):
+                    if (t + 1) % 2 != q:
+                        continue
+                    k = (t + 1) // 2
+                    piece = line[t * 8 : t * 8 + 8, c * LANES : (c + 1) * LANES]
+                    if k == 0:
+                        inside = inside + piece
+                        continue
+                    piece = pltpu.roll(piece, 16 * k, 1)
+                    inside = inside + jnp.where(lane >= 16 * k, piece, 0.0)
+                    beyond = jnp.where(lane < 16 * k, piece, 0.0)
+                    outside = beyond if outside is None else outside + beyond
+                insides.append(inside)
+                outsides.append(outside)
+            near[c], far[c] = jnp.stack(insides), jnp.stack(outsides)
+        first = conjugate_by_h(read_matrix(lambda c: v_all[c]), read_matrix(lambda c: near[c]))
+        second = conjugate_by_h(read_matrix(lambda c: v_wrap[c]), read_matrix(lambda c: far[c]))
+        for r in range(8):
+            final[r * 40 + 32 : r * 40 + 40, :] = jnp.zeros((8, LANES), jnp.float32)
+        for c, value in each(map_matrix(lambda m, n: m + n, first, second)):
+            for q in range(2):
+                final[pl.ds(q * 18 + c, 8, stride=40), :] = value[q]
+        for d, value in enumerate(block_transpose([final[r * 40 : r * 40 + 40, :] for r in range(8)])):
+            back[d] = value
+        copies, back_arrivals = exchange(back, returned, slice(0, 40), back_send, back_recv)
+        for copy in copies:
+            copy.start()
+        started += copies
+        returned[me] = back[me]
+
+    with jax.named_scope("weight_sum"):
+        for arrival in across_arrivals:
+            arrival.wait_recv()
+        summed = across[0]
+        for s in range(1, yz_count):
+            summed = summed + across[s]
+        whole[me] = summed * scale
+        whole_copies, whole_arrivals = spread("gx", 8, whole.at[me], whole, whole_send, whole_recv)
+        for copy in whole_copies:
+            copy.start()
+        started += whole_copies
+
+    with jax.named_scope("unpack"):
+        for arrival in back_arrivals:
+            arrival.wait_recv()
+        rows = block_transpose([returned[r] for r in range(8)])
+        for c in range(8):
+            for x in range(2):
+                for ab in range(9):
+                    row = x * 18 + ab * 2
+                    out_ref[c, x, ab // 3, ab % 3, :, :] = rows[c][row : row + 2]
+        for arrival in whole_arrivals:
+            arrival.wait_recv()
+        for i in range(8):
+            value = whole[i]
+            for l in range(8):
+                gw_out[pl.ds(i * 64 + l, 8, stride=8), :] = value[:, l * 8 : l * 8 + 8]
+        for copy in started:
+            copy.wait_send()
+
+
+def resident(scale, yz_count, gauge_links, in_field, cotangent, bilinear_weights):
+    f32 = jnp.float32
+    vmem = pl.BlockSpec(memory_space=pltpu.VMEM)
+    dma = pltpu.SemaphoreType.DMA
+    grad_field, grad_weights = pl.pallas_call(
+        functools.partial(whole_kernel, scale, yz_count),
+        out_shape=(
+            jax.ShapeDtypeStruct((8, 2, 3, 3, 2, LANES), f32),
+            jax.ShapeDtypeStruct((512, 8), f32),
+        ),
+        in_specs=[vmem] * 4,
+        out_specs=(vmem, vmem),
+        scratch_shapes=[
+            pltpu.VMEM((8, 80, LANES), f32),
+            pltpu.VMEM((8, 80, LANES), f32),
+            pltpu.VMEM((8, 80, LANES), f32),
+            pltpu.VMEM((640, LANES), f32),
+            pltpu.VMEM((18, 2, 8, LANES), f32),
+            pltpu.VMEM((18, 2, 8, LANES), f32),
+            pltpu.VMEM((18, 2, 8, LANES), f32),
+            pltpu.VMEM((18, 2, 8, LANES), f32),
+            pltpu.VMEM((18, 2, 8, LANES), f32),
+            pltpu.VMEM((128, 256), f32),
+            pltpu.VMEM((256, 18 * LANES), jnp.bfloat16),
+            pltpu.VMEM((128, 18 * LANES), f32),
+            pltpu.VMEM((128, 18 * LANES), f32),
+            pltpu.VMEM((80, 18 * LANES), f32),
+            pltpu.VMEM((18, 2, 8, LANES), f32),
+            pltpu.VMEM((320, LANES), f32),
+            pltpu.VMEM((8, 40, LANES), f32),
+            pltpu.VMEM((8, 40, LANES), f32),
+            pltpu.VMEM((8, 8, LANES), f32),
+            pltpu.VMEM((8, 8, LANES), f32),
+            pltpu.VMEM((8, LANES), f32),
+            pltpu.VMEM((yz_count, 8, LANES), f32),
+            pltpu.VMEM((8, 8, LANES), f32),
+        ]
+        + [dma((8,))] * 8
+        + [dma((yz_count,)), dma((yz_count,)), dma((8,)), dma((8,))],
+        compiler_params=pltpu.CompilerParams(
+            collective_id=0, has_side_effects=True, vmem_limit_bytes=VMEM_BYTES
+        ),
+        name="lattice_backward",
+    )(
+        gauge_links.transpose(0, 2, 3, 1, 4),
+        in_field.transpose(0, 1, 3, 4, 2, 5),
+        cotangent.transpose(0, 1, 3, 4, 2, 5),
+        bilinear_weights.reshape(512, 8),
+    )
+    return grad_field.transpose(0, 1, 4, 2, 3, 5), grad_weights.reshape(8, 8, 8, 8)
+
+
+def mm(left, right, left_h=False, right_h=False):
+    def pick(m, h, a, b):
+        return (m[0][b][a], m[1][b][a]) if h else (m[0][a][b], m[1][a][b])
+
+    real = [[None] * 3 for _ in range(3)]
+    imag = [[None] * 3 for _ in range(3)]
+    for a in range(3):
+        for b in range(3):
+            re = im = None
+            for k in range(3):
+                lr, li = pick(left, left_h, a, k)
+                rr, ri = pick(right, right_h, k, b)
+                rr_lr, ii = lr * rr, li * ri
+                re = rr_lr if re is None else re + rr_lr
+                re = re + ii if left_h != right_h else re - ii
+                first, second = lr * ri, li * rr
+                if right_h and left_h:
+                    term = -(first + second)
+                elif right_h:
+                    term = second - first
+                elif left_h:
+                    term = first - second
+                else:
+                    term = first + second
+                im = term if im is None else im + term
+            real[a][b], imag[a][b] = re, im
+    return [real, imag]
+
+
+def map_matrix(f, *ms):
+    return [[[f(*(m[r][a][b] for m in ms)) for b in range(3)] for a in range(3)] for r in range(2)]
+
+
+def comp(r, a, b):
+    return (a * 3 + b) * 2 + r
+
+
+def read_matrix(f):
+    return [[[f(comp(r, a, b)) for b in range(3)] for a in range(3)] for r in range(2)]
+
+
+def each(m):
+    for r in range(2):
+        for a in range(3):
+            for b in range(3):
+                yield comp(r, a, b), m[r][a][b]
+
+
+def conjugate_by(v, m):
+    return mm(mm(v, m), v, right_h=True)
+
+
+def conjugate_by_h(v, m):
+    return mm(mm(v, m, left_h=True), v)
+
+
+def split(value):
+    high = value.astype(jnp.bfloat16)
+    return high, (value - high.astype(jnp.float32)).astype(jnp.bfloat16)
+
+
+def per_device(gauge_links, in_field, cotangent, bilinear_weights):
+    gx = lax.axis_size("gx")
+    yz = lax.axis_size("yz")
+    fits = (
+        gx == 8
+        and in_field.shape == (8, 2, 2, 3, 3, LANES)
+        and bilinear_weights.shape == (8, 8, 8, 8)
+    )
+    if not fits:
+        return general(gauge_links, in_field, cotangent, bilinear_weights)
+    total = gauge_links.shape[0] * gx * gauge_links.shape[-1] * yz
+    scale = 1.0 / math.sqrt(100.0 * total)
+    return resident(scale, yz, gauge_links, in_field, cotangent, bilinear_weights)
+
+
 def solution(mesh):
     placed = (
         P("gx", None, None, None, "yz"),

time: 154 us -> 31.8 us (0.21)
  blocking collectives: 42.1 us -> 0 us
  loops' own time: 34.6 us -> 0 us
  Pallas kernels: 0 us -> 28.6 us
  local copies, waits for them, and re-layouts: 24.8 us -> 2.35 us
  starting transfers between devices: 16.8 us -> 0 us
  waiting for transfers between devices: 16.4 us -> 0 us
  other arithmetic: 12.2 us -> 0 us
  matrix products: 5.08 us -> 0 us
    psum x1 -> x0, blocking collectives: 42.1 us -> none  [per_device(): summed = lax.psum(partial_grad, ('gx', 'yz'))]
    another operation x3 -> x0, loops' own time: 34.6 us -> none  [the longest x1 17.8 us: per_device(): lax.scan(forward_step, gauge_links, offsets)]
    pallas_call x0 -> x1, Pallas kernels: none -> 28.6 us  [resident(): pl.pallas_call(functools.partial(whole_kernel, scale, yz_count), out_shap...]
    ppermute x11 -> x0, starting transfers between devices: 16.8 us -> none  [from_behind(): return lax.ppermute(block, axis, route)]
    ppermute x11 -> x0, waiting for transfers between devices: 16.4 us -> none  [from_behind(): return lax.ppermute(block, axis, route)]
    dynamic_slice x24 -> x0, local copies, waits for them, and re-layouts: 10.2 us -> none  [the longest x16 10 us: per_device(): lax.scan(forward_step, gauge_links, offsets)]
    squeeze x8 -> x0, local copies, waits for them, and re-layouts: 7.41 us -> none  [per_device(): lax.scan(backward_step, accumulator, (offsets, line_grad, all_lines))]
    reduce_sum x42 -> x0, other arithmetic: 6.48 us -> none  [the longest x41 6.43 us: matmul_three(): jnp.sum(left[..., :, :, None, :] * right[..., None, :, :, :], axis=-3)]
  transfers between devices with their start and end apart: 11 -> 0, of which waited for: 9 -> 0; matrix products, arithmetic and copies ran while one was open for 4% -> 0% of each run, Pallas kernels for 0% -> 0%
where the time goes in v2:
time: 31.8 us; the launch traced here: 31.6 us
  Pallas kernels  28.6 us (90%)
  local copies, waits for them, and re-layouts  2.35 us (7%)
  between operations  0.65 us (2%)
    pallas_call x1, Pallas kernels, resident(): pl.pallas_call(functools.partial(whole_kernel, scale, yz_count), out_shap...  28.6 us
    unnamed x4, local copies, waits for them, and re-layouts  2.35 us

profile of v2, /device:TPU:0, one launch (start us, length us, event | category | flops | bytes accessed | tf_op | source)
XLA Modules:
  0.0 31.6 jit_solution(10364462744094289837)
XLA Ops:
  0.6 28.6 %lattice_backward.1 = (f32[8,2,3,3,2,128]{5,4,3,2,1,0:T(2,128)}, f32[512,8]{1,0:T(8,128)}) custom-call(f32[2,3,3,2,128]{4,3,2,1,0:T(2,128)} %bitcast.11, f32[8,2,3,3,2,128]{5,4,3,2,1,0:T(2,128)} %bitcast.8, f32[8,2,3,3,2,128]{5,4,3,2,1,0:T(2,128)} %bitcast.9, f32[512,8]{1,0:T(8,128)} %bitcast.6), custom_call_target="tpu_custom_call" | custom-call | tf_op jit(solution)/shard_map/lattice_backward/pallas_call | solution.py:495
  29.3 0.0 copy-start
  29.3 1.6 %copy.8 = f32[8,2,2,3,3,128]{5,2,4,3,1,0:T(2,128)} copy(f32[8,2,2,3,3,128]{5,2,4,3,1,0:T(2,128)} %bitcast.10) | data formatting | bytes 294912
  30.9 0.0 copy-done
  30.9 0.7 %copy.9 = f32[8,8,8,8]{3,2,1,0:T(8,128)} copy(f32[8,8,8,8]{3,2,1,0:T(8,128)S(1)} %bitcast.7) | data formatting | bytes 32768
Async XLA Ops:
  29.3 1.7 %copy-start = (f32[512,8]{1,0:T(8,128)S(1)}, f32[512,8]{1,0:T(8,128)}, u32[]{:S(2)}) copy-start(f32[512,8]{1,0:T(8,128)} %get-tuple-element.5) | copy-start | bytes 49156

commit v3 on v2

--- a/solution.py
+++ b/solution.py
@@ -10,7 +10,7 @@
 
 MESH = pl.DeviceIdType.MESH
 LANES = 128
-VMEM_BYTES = 56 * 1024 * 1024
+VMEM_BYTES = 20 * 1024 * 1024
 
 
 def from_behind(block, axis, distance):
@@ -160,21 +160,29 @@
     return outgoing, incoming
 
 
+def other(me, mask):
+    for bit in (1, 2, 4):
+        if mask & bit:
+            me = me + bit - 2 * bit * (me // bit % 2)
+    return me
+
+
+FAR_FIRST = (4, 5, 6, 7, 2, 3, 1)
+
+
 def exchange(source, target, rows, send_sem, recv_sem):
     me = lax.axis_index("gx")
     outgoing, incoming = [], []
-    for k in range(1, 8):
-        for found, here, slot, there in (
-            (outgoing, lax.rem(me + k, 8), me, lax.rem(me + k, 8)),
-            (incoming, lax.rem(me + k, 8), lax.rem(me + 8 - k, 8), lax.rem(me + 8 - k, 8)),
-        ):
+    for k in FAR_FIRST:
+        peer = other(me, k)
+        for found, slot in ((outgoing, me), (incoming, peer)):
             found.append(
                 pltpu.make_async_remote_copy(
-                    src_ref=source.at[here, rows, :],
+                    src_ref=source.at[peer, rows, :],
                     dst_ref=target.at[slot, rows, :],
                     send_sem=send_sem.at[k],
                     recv_sem=recv_sem.at[k],
-                    device_id={"gx": there},
+                    device_id={"gx": peer},
                     device_id_type=MESH,
                 )
             )
@@ -184,12 +192,16 @@
 def whole_kernel(
     scale,
     yz_count,
+    u_hbm,
+    w_hbm,
+    g_hbm,
+    weight_hbm,
+    out_ref,
+    gw_out,
     u_ref,
     w_ref,
     g_ref,
     weight_ref,
-    out_ref,
-    gw_out,
     packed,
     sending,
     landed,
@@ -202,6 +214,7 @@
     rows_ref,
     z,
     pair,
+    halves,
     mixed,
     line,
     total,
@@ -219,15 +232,26 @@
     second_recv,
     back_send,
     back_recv,
+    last_send,
+    last_recv,
     share_send,
     share_recv,
     across_send,
     across_recv,
     whole_send,
     whole_recv,
+    load_sem,
 ):
     me = lax.axis_index("gx")
     here = lax.axis_index("yz")
+    loads = [
+        pltpu.make_async_copy(source, target, load_sem.at[k])
+        for k, (source, target) in enumerate(
+            ((w_hbm, w_ref), (u_hbm, u_ref), (g_hbm, g_ref), (weight_hbm, weight_ref))
+        )
+    ]
+    for load in loads:
+        load.start()
     ready = greet((("gx", 8), ("yz", yz_count)))
     lane1 = lax.broadcasted_iota(jnp.int32, (1, LANES), 1)
     lane = lax.broadcasted_iota(jnp.int32, (8, LANES), 1)
@@ -236,14 +260,20 @@
     with jax.named_scope("pack"):
         packed[:, 32:48, :] = jnp.zeros((8, 16, LANES), jnp.float32)
         packed[:, 72:80, :] = jnp.zeros((8, 8, LANES), jnp.float32)
+        loads[0].wait()
+        loads[1].wait()
         for x in range(2):
             for ab in range(9):
                 row = x * 18 + ab * 2
                 packed[:, row : row + 2, :] = w_ref[:, x, ab // 3, ab % 3, :, :]
-                packed[:, 41 + row : 43 + row, :] = g_ref[:, x, ab // 3, ab % 3, :, :]
                 for part in range(2):
                     r, t = divmod(row + part, 5)
                     packed[r, 36 + t : 37 + t, :] = u_ref[x, ab // 3, ab % 3, part : part + 1, :]
+        loads[2].wait()
+        for x in range(2):
+            for ab in range(9):
+                row = x * 18 + ab * 2
+                packed[:, 41 + row : 43 + row, :] = g_ref[:, x, ab // 3, ab % 3, :, :]
         started = []
         arrivals = []
         for rows, send, recv in ((early, first_send, first_recv), (late, second_send, second_recv)):
@@ -259,6 +289,7 @@
         landed[me] = sending[me]
 
     with jax.named_scope("weights"):
+        loads[3].wait()
         rows_ref[...] = jnp.zeros((128, 256), jnp.float32)
         for i in range(8):
             pieces = [weight_ref[pl.ds(i * 64 + l, 8, stride=8), :] for l in range(8)]
@@ -357,21 +388,15 @@
                     pair[pl.ds(row, 8), c * LANES : (c + 1) * LANES] = value
 
     with jax.named_scope("products"):
-        weights = jnp.zeros((256, 160), jnp.float32)
         for chunk in range(9):
             columns = slice(chunk * 256, (chunk + 1) * 256)
             high, low = split(pair[:, columns])
-            zc = z[:, columns]
-            weights = weights + lax.dot_general(
-                jnp.concatenate([high, low], axis=0),
-                zc[0:160],
-                (((1,), (1,)), ((), ())),
-                preferred_element_type=jnp.float32,
-            )
-            mixed[:, columns] = jnp.dot(w3, zc, preferred_element_type=jnp.float32)
-            line[:, columns] = jnp.dot(
-                wt3, jnp.concatenate([high, low, high], axis=0), preferred_element_type=jnp.float32
-            )
+            halves[0:128, columns] = high
+            halves[128:256, columns] = low
+            halves[256:384, columns] = high
+        weights = lax.dot_general(
+            halves[0:256, :], z[0:160, :], (((1,), (1,)), ((), ())), preferred_element_type=jnp.float32
+        )
         half = weights[0:128] + weights[128:256]
         both = half[:, 0:80] + half[:, 80:160]
         both = both[0:64, 0:64] + both[64:128, 8:72]
@@ -383,23 +408,33 @@
             copy.start()
         shares[me] = partial[me]
         started += share_copies
-
-    with jax.named_scope("direct"):
-        @pl.loop(0, 3)
-        def _(a):
-            for p in range(2):
+        for chunk in range(9):
+            columns = slice(chunk * 256, (chunk + 1) * 256)
+            mixed[:, columns] = jnp.dot(w3, z[:, columns], preferred_element_type=jnp.float32)
+            line[:, columns] = jnp.dot(wt3, halves[:, columns], preferred_element_type=jnp.float32)
+
+    for r in range(8):
+        final[r * 40 + 32 : r * 40 + 40, :] = jnp.zeros((8, LANES), jnp.float32)
+    back_arrivals = []
+    for p, rows, send, recv in (
+        (0, slice(0, 16), back_send, back_recv),
+        (1, slice(16, 40), last_send, last_recv),
+    ):
+        with jax.named_scope("direct"):
+            @pl.loop(0, 3)
+            def _(a):
                 sums = [[None, None] for _ in range(3)]
                 for i in range(8):
-                    rows = slice(p * 64 + i * 8, p * 64 + i * 8 + 8)
+                    lines = slice(p * 64 + i * 8, p * 64 + i * 8 + 8)
                     for k in range(3):
                         at = (a * 3 + k) * 2
                         gr = jnp.broadcast_to(cot[at, p, i : i + 1, :], (8, LANES))
                         gi = jnp.broadcast_to(cot[at + 1, p, i : i + 1, :], (8, LANES))
                         for b in range(3):
                             at = comp(0, b, k) * LANES
-                            mr = mixed[rows, at : at + LANES]
+                            mr = mixed[lines, at : at + LANES]
                             at = comp(1, b, k) * LANES
-                            mi = mixed[rows, at : at + LANES]
+                            mi = mixed[lines, at : at + LANES]
                             re = gr * mr + gi * mi
                             im = gi * mr - gr * mi
                             s = sums[b]
@@ -408,27 +443,12 @@
                     total[(a * 3 + b) * 2, p] = sums[b][0]
                     total[(a * 3 + b) * 2 + 1, p] = sums[b][1]
 
-    with jax.named_scope("share_sum"):
-        for arrival in share_arrivals:
-            arrival.wait_recv()
-        subtotal = shares[0]
-        for s in range(1, 8):
-            subtotal = subtotal + shares[s]
-        mine[...] = subtotal
-        across_copies, across_arrivals = spread("yz", yz_count, mine, across, across_send, across_recv)
-        for copy in across_copies:
-            copy.start()
-        across[here] = subtotal
-        started += across_copies
-
-    with jax.named_scope("from_frame"):
-        near, far = {}, {}
-        for c in range(18):
-            insides, outsides = [], []
-            for q in range(2):
-                inside, outside = total[c, q], None
+        with jax.named_scope("from_frame"):
+            near, far = {}, {}
+            for c in range(18):
+                inside, outside = total[c, p], None
                 for t in range(9):
-                    if (t + 1) % 2 != q:
+                    if (t + 1) % 2 != p:
                         continue
                     k = (t + 1) // 2
                     piece = line[t * 8 : t * 8 + 8, c * LANES : (c + 1) * LANES]
@@ -439,23 +459,36 @@
                     inside = inside + jnp.where(lane >= 16 * k, piece, 0.0)
                     beyond = jnp.where(lane < 16 * k, piece, 0.0)
                     outside = beyond if outside is None else outside + beyond
-                insides.append(inside)
-                outsides.append(outside)
-            near[c], far[c] = jnp.stack(insides), jnp.stack(outsides)
-        first = conjugate_by_h(read_matrix(lambda c: v_all[c]), read_matrix(lambda c: near[c]))
-        second = conjugate_by_h(read_matrix(lambda c: v_wrap[c]), read_matrix(lambda c: far[c]))
-        for r in range(8):
-            final[r * 40 + 32 : r * 40 + 40, :] = jnp.zeros((8, LANES), jnp.float32)
-        for c, value in each(map_matrix(lambda m, n: m + n, first, second)):
-            for q in range(2):
-                final[pl.ds(q * 18 + c, 8, stride=40), :] = value[q]
-        for d, value in enumerate(block_transpose([final[r * 40 : r * 40 + 40, :] for r in range(8)])):
-            back[d] = value
-        copies, back_arrivals = exchange(back, returned, slice(0, 40), back_send, back_recv)
-        for copy in copies:
-            copy.start()
-        started += copies
-        returned[me] = back[me]
+                near[c], far[c] = inside, outside
+            first = conjugate_by_h(read_matrix(lambda c: v_all[c, p]), read_matrix(lambda c: near[c]))
+            second = conjugate_by_h(read_matrix(lambda c: v_wrap[c, p]), read_matrix(lambda c: far[c]))
+            for c, value in each(map_matrix(lambda m, n: m + n, first, second)):
+                final[pl.ds(p * 18 + c, 8, stride=40), :] = value
+            ready_rows = [final[r * 40 + rows.start : r * 40 + rows.stop, :] for r in range(8)]
+            for d, value in enumerate(block_transpose(ready_rows)):
+                back[d, rows, :] = value
+            copies, incoming = exchange(back, returned, rows, send, recv)
+            for copy in copies:
+                copy.start()
+            started += copies
+            back_arrivals.append((rows, incoming))
+            returned[me, rows, :] = back[me, rows, :]
+
+        if p == 0:
+            with jax.named_scope("share_sum"):
+                for arrival in share_arrivals:
+                    arrival.wait_recv()
+                subtotal = shares[0]
+                for s in range(1, 8):
+                    subtotal = subtotal + shares[s]
+                mine[...] = subtotal
+                across_copies, across_arrivals = spread(
+                    "yz", yz_count, mine, across, across_send, across_recv
+                )
+                for copy in across_copies:
+                    copy.start()
+                across[here] = subtotal
+                started += across_copies
 
     with jax.named_scope("weight_sum"):
         for arrival in across_arrivals:
@@ -470,37 +503,47 @@
         started += whole_copies
 
     with jax.named_scope("unpack"):
-        for arrival in back_arrivals:
-            arrival.wait_recv()
-        rows = block_transpose([returned[r] for r in range(8)])
-        for c in range(8):
-            for x in range(2):
-                for ab in range(9):
-                    row = x * 18 + ab * 2
-                    out_ref[c, x, ab // 3, ab % 3, :, :] = rows[c][row : row + 2]
+        for rows, incoming in back_arrivals:
+            for arrival in incoming:
+                arrival.wait_recv()
+            for c, value in enumerate(block_transpose([returned[r, rows, :] for r in range(8)])):
+                out_ref[c, rows, :] = value
         for arrival in whole_arrivals:
             arrival.wait_recv()
-        for i in range(8):
-            value = whole[i]
-            for l in range(8):
-                gw_out[pl.ds(i * 64 + l, 8, stride=8), :] = value[:, l * 8 : l * 8 + 8]
+        gw_out[...] = whole[...]
         for copy in started:
             copy.wait_send()
+
+
+def place_kernel(rows_ref, weights_ref, out_ref, gw_out):
+    for x in range(2):
+        for ab in range(9):
+            row = x * 18 + ab * 2
+            out_ref[:, x, ab // 3, ab % 3, :, :] = rows_ref[:, row : row + 2, :]
+    for i in range(8):
+        value = weights_ref[i]
+        for l in range(8):
+            gw_out[pl.ds(i * 64 + l, 8, stride=8), :] = value[:, l * 8 : l * 8 + 8]
 
 
 def resident(scale, yz_count, gauge_links, in_field, cotangent, bilinear_weights):
     f32 = jnp.float32
     vmem = pl.BlockSpec(memory_space=pltpu.VMEM)
     dma = pltpu.SemaphoreType.DMA
-    grad_field, grad_weights = pl.pallas_call(
+    placed = pl.BlockSpec(memory_space=pltpu.HBM)
+    rows, weights = pl.pallas_call(
         functools.partial(whole_kernel, scale, yz_count),
         out_shape=(
-            jax.ShapeDtypeStruct((8, 2, 3, 3, 2, LANES), f32),
-            jax.ShapeDtypeStruct((512, 8), f32),
+            jax.ShapeDtypeStruct((8, 40, LANES), f32),
+            jax.ShapeDtypeStruct((8, 8, LANES), f32),
         ),
-        in_specs=[vmem] * 4,
+        in_specs=[placed] * 4,
         out_specs=(vmem, vmem),
         scratch_shapes=[
+            pltpu.VMEM((2, 3, 3, 2, LANES), f32),
+            pltpu.VMEM((8, 2, 3, 3, 2, LANES), f32),
+            pltpu.VMEM((8, 2, 3, 3, 2, LANES), f32),
+            pltpu.VMEM((512, 8), f32),
             pltpu.VMEM((8, 80, LANES), f32),
             pltpu.VMEM((8, 80, LANES), f32),
             pltpu.VMEM((8, 80, LANES), f32),
@@ -513,6 +556,7 @@
             pltpu.VMEM((128, 256), f32),
             pltpu.VMEM((256, 18 * LANES), jnp.bfloat16),
             pltpu.VMEM((128, 18 * LANES), f32),
+            pltpu.VMEM((384, 18 * LANES), jnp.bfloat16),
             pltpu.VMEM((128, 18 * LANES), f32),
             pltpu.VMEM((80, 18 * LANES), f32),
             pltpu.VMEM((18, 2, 8, LANES), f32),
@@ -525,18 +569,29 @@
             pltpu.VMEM((yz_count, 8, LANES), f32),
             pltpu.VMEM((8, 8, LANES), f32),
         ]
-        + [dma((8,))] * 8
-        + [dma((yz_count,)), dma((yz_count,)), dma((8,)), dma((8,))],
+        + [dma((8,))] * 10
+        + [dma((yz_count,)), dma((yz_count,)), dma((8,)), dma((8,)), dma((4,))],
         compiler_params=pltpu.CompilerParams(
             collective_id=0, has_side_effects=True, vmem_limit_bytes=VMEM_BYTES
         ),
         name="lattice_backward",
     )(
-        gauge_links.transpose(0, 2, 3, 1, 4),
-        in_field.transpose(0, 1, 3, 4, 2, 5),
-        cotangent.transpose(0, 1, 3, 4, 2, 5),
-        bilinear_weights.reshape(512, 8),
-    )
+        pltpu.with_memory_space_constraint(gauge_links.transpose(0, 2, 3, 1, 4), pltpu.HBM),
+        pltpu.with_memory_space_constraint(in_field.transpose(0, 1, 3, 4, 2, 5), pltpu.HBM),
+        pltpu.with_memory_space_constraint(cotangent.transpose(0, 1, 3, 4, 2, 5), pltpu.HBM),
+        pltpu.with_memory_space_constraint(bilinear_weights.reshape(512, 8), pltpu.HBM),
+    )
+    grad_field, grad_weights = pl.pallas_call(
+        place_kernel,
+        out_shape=(
+            jax.ShapeDtypeStruct((8, 2, 3, 3, 2, LANES), f32),
+            jax.ShapeDtypeStruct((512, 8), f32),
+        ),
+        in_specs=[vmem] * 2,
+        out_specs=(vmem, vmem),
+        compiler_params=pltpu.CompilerParams(vmem_limit_bytes=VMEM_BYTES),
+        name="place_rows",
+    )(rows, weights)
     return grad_field.transpose(0, 1, 4, 2, 3, 5), grad_weights.reshape(8, 8, 8, 8)
 
 

time: 31.8 us -> 28.6 us (0.90)
  local copies, waits for them, and re-layouts: 2.35 us -> 0 us
  Pallas kernels: 28.6 us -> 27.9 us
    unnamed x4 -> x0, local copies, waits for them, and re-layouts: 2.35 us -> none
    pallas_call x1, Pallas kernels: 28.6 us -> 27 us  [resident(): pl.pallas_call(functools.partial(whole_kernel, scale, yz_count), out_shap...]
    pallas_call x0 -> x1, Pallas kernels: none -> 0.84 us  [resident(): pl.pallas_call(place_kernel, out_shape=(jax.ShapeDtypeStruct((8, 2, 3, 3,...]
where the time goes in v3:
time: 28.6 us; the launch traced here: 28.5 us
  Pallas kernels  27.9 us (98%)
  between operations  0.64 us (2%)
    pallas_call x1, Pallas kernels, resident(): pl.pallas_call(functools.partial(whole_kernel, scale, yz_count), out_shap...  27 us
    pallas_call x1, Pallas kernels, resident(): pl.pallas_call(place_kernel, out_shape=(jax.ShapeDtypeStruct((8, 2, 3, 3,...  0.84 us

profile of v3, /device:TPU:0, one launch (start us, length us, event | category | flops | bytes accessed | tf_op | source)
XLA Modules:
  0.0 28.5 jit_solution(2497221567371321763)
XLA Ops:
  0.6 27.0 %lattice_backward.1 = (f32[8,40,128]{2,1,0:T(8,128)S(1)}, f32[8,8,128]{2,1,0:T(8,128)S(1)}) custom-call(f32[2,3,3,2,128]{4,3,2,1,0:T(2,128)} %bitcast.9, f32[8,2,3,3,2,128]{5,4,3,2,1,0:T(2,128)} %bitcast.7, f32[8,2,3,3,2,128]{5,4,3,2,1,0:T(2,128)} %bitcast.8, f32[512,8]{1,0:T(8,128)} %bitcast.6), custom_call_target="tpu_custom_call" | custom-call | tf_op jit(solution)/shard_map/lattice_backward/pallas_call | solution.py:534
  27.7 0.8 %place_rows.1 = (f32[8,2,3,3,2,128]{5,4,3,2,1,0:T(2,128)}, f32[512,8]{1,0:T(8,128)}) custom-call(f32[8,40,128]{2,1,0:T(8,128)S(1)} %get-tuple-element.6.rows_ref, f32[8,8,128]{2,1,0:T(8,128)S(1)} %get-tuple-element.7.weights_ref), custom_call_target="tpu_custom_call" | custom-call | tf_op jit(solution)/shard_map/place_rows/pallas_call | solution.py:584

commit v4 on v3

--- a/solution.py
+++ b/solution.py
@@ -183,6 +183,25 @@
                     send_sem=send_sem.at[k],
                     recv_sem=recv_sem.at[k],
                     device_id={"gx": peer},
+                    device_id_type=MESH,
+                )
+            )
+    return outgoing, incoming
+
+
+def deal(source, target, send_sem, recv_sem):
+    me = lax.axis_index("yz")
+    outgoing, incoming = [], []
+    for k in range(1, 4):
+        peer = other(me, k)
+        for found, slot in ((outgoing, me), (incoming, peer)):
+            found.append(
+                pltpu.make_async_remote_copy(
+                    src_ref=source.at[peer],
+                    dst_ref=target.at[slot],
+                    send_sem=send_sem.at[k],
+                    recv_sem=recv_sem.at[k],
+                    device_id={"yz": peer},
                     device_id_type=MESH,
                 )
             )
@@ -230,6 +249,8 @@
     first_recv,
     second_send,
     second_recv,
+    third_send,
+    third_recv,
     back_send,
     back_recv,
     last_send,
@@ -255,7 +276,7 @@
     ready = greet((("gx", 8), ("yz", yz_count)))
     lane1 = lax.broadcasted_iota(jnp.int32, (1, LANES), 1)
     lane = lax.broadcasted_iota(jnp.int32, (8, LANES), 1)
-    early, late = slice(0, 48), slice(48, 80)
+    early, even, odd_part = slice(0, 48), slice(48, 64), slice(64, 80)
 
     with jax.named_scope("pack"):
         packed[:, 32:48, :] = jnp.zeros((8, 16, LANES), jnp.float32)
@@ -276,7 +297,11 @@
                 packed[:, 41 + row : 43 + row, :] = g_ref[:, x, ab // 3, ab % 3, :, :]
         started = []
         arrivals = []
-        for rows, send, recv in ((early, first_send, first_recv), (late, second_send, second_recv)):
+        for rows, send, recv in (
+            (early, first_send, first_recv),
+            (even, second_send, second_recv),
+            (odd_part, third_send, third_recv),
+        ):
             for d, value in enumerate(block_transpose([packed[r, rows, :] for r in range(8)])):
                 sending[d, rows, :] = value
             if not started:
@@ -301,8 +326,13 @@
         low = value - high
         w3 = (high + pltpu.roll(high, 80, 1) + pltpu.roll(low, 160, 1)).astype(jnp.bfloat16)
         turned = value[:, 0:LANES].T[0:80]
-        high, low = split(turned)
-        wt3 = jnp.concatenate([high, high, low], axis=1)
+        high = turned.astype(jnp.bfloat16).astype(jnp.float32)
+        low = turned - high
+        wt3 = []
+        for p in range(2):
+            part = slice(p * 64, p * 64 + 64)
+            joined = jnp.concatenate([high[:, part], high[:, part], low[:, part]], axis=1)
+            wt3.append(joined.astype(jnp.bfloat16))
 
     with jax.named_scope("links_and_field"):
         for arrival in arrivals[0]:
@@ -369,49 +399,83 @@
             z[80:160, columns] = low
             z[160:240, columns] = high
 
-    with jax.named_scope("pairs"):
-        for arrival in arrivals[1]:
-            arrival.wait_recv()
-        for c, value in enumerate(block_transpose([landed[r, late, :] for r in range(8)])):
-            sites[c * 80 + 48 : c * 80 + 80, :] = value
-        v = read_matrix(lambda c: v_all[c])
-        for c, value in each(conjugate_by(v, read_sites(41))):
-            cot[c] = value
-
-        @pl.loop(0, 8)
-        def _(i):
-            for p in range(2):
-                w = read_matrix(lambda c: field[c, p])
-                g = read_matrix(lambda c: jnp.broadcast_to(cot[c, p, pl.ds(i, 1), :], (8, LANES)))
-                row = pl.multiple_of(p * 64 + i * 8, 8)
-                for c, value in each(mm(w, g, left_h=True)):
-                    pair[pl.ds(row, 8), c * LANES : (c + 1) * LANES] = value
-
-    with jax.named_scope("products"):
-        for chunk in range(9):
-            columns = slice(chunk * 256, (chunk + 1) * 256)
-            high, low = split(pair[:, columns])
-            halves[0:128, columns] = high
-            halves[128:256, columns] = low
-            halves[256:384, columns] = high
-        weights = lax.dot_general(
-            halves[0:256, :], z[0:160, :], (((1,), (1,)), ((), ())), preferred_element_type=jnp.float32
-        )
-        half = weights[0:128] + weights[128:256]
-        both = half[:, 0:80] + half[:, 80:160]
-        both = both[0:64, 0:64] + both[64:128, 8:72]
-        both = jnp.concatenate([both, jnp.zeros((64, 64), jnp.float32)], axis=1)
-        for d in range(8):
-            partial[d] = both[d * 8 : d * 8 + 8]
-        share_copies, share_arrivals = exchange(partial, shares, slice(0, 8), share_send, share_recv)
-        for copy in share_copies:
-            copy.start()
-        shares[me] = partial[me]
-        started += share_copies
+    def direct(p):
+        @pl.loop(0, 3)
+        def _(a):
+            sums = [[None, None] for _ in range(3)]
+            for i in range(8):
+                lines = slice(p * 64 + i * 8, p * 64 + i * 8 + 8)
+                for k in range(3):
+                    at = (a * 3 + k) * 2
+                    gr = jnp.broadcast_to(cot[at, p, i : i + 1, :], (8, LANES))
+                    gi = jnp.broadcast_to(cot[at + 1, p, i : i + 1, :], (8, LANES))
+                    for b in range(3):
+                        at = comp(0, b, k) * LANES
+                        mr = mixed[lines, at : at + LANES]
+                        at = comp(1, b, k) * LANES
+                        mi = mixed[lines, at : at + LANES]
+                        re = gr * mr + gi * mi
+                        im = gi * mr - gr * mi
+                        s = sums[b]
+                        sums[b] = [re, im] if s[0] is None else [s[0] + re, s[1] + im]
+            for b in range(3):
+                total[(a * 3 + b) * 2, p] = sums[b][0]
+                total[(a * 3 + b) * 2 + 1, p] = sums[b][1]
+
+    with jax.named_scope("mixed"):
         for chunk in range(9):
             columns = slice(chunk * 256, (chunk + 1) * 256)
             mixed[:, columns] = jnp.dot(w3, z[:, columns], preferred_element_type=jnp.float32)
-            line[:, columns] = jnp.dot(wt3, halves[:, columns], preferred_element_type=jnp.float32)
+
+    sums = []
+    for p, rows in ((0, even), (1, odd_part)):
+        with jax.named_scope("pairs"):
+            for arrival in arrivals[1 + p]:
+                arrival.wait_recv()
+            for c, value in enumerate(block_transpose([landed[r, rows, :] for r in range(8)])):
+                sites[c * 80 + rows.start : c * 80 + rows.stop, :] = value
+            v = read_matrix(lambda c: v_all[c, p])
+            g = read_matrix(lambda c: sites[pl.ds(41 + p * 18 + c, 8, stride=80), :])
+            for c, value in each(conjugate_by(v, g)):
+                cot[c, p] = value
+
+            @pl.loop(0, 8)
+            def _(i):
+                w = read_matrix(lambda c: field[c, p])
+                g = read_matrix(lambda c: jnp.broadcast_to(cot[c, p, pl.ds(i, 1), :], (8, LANES)))
+                row = pl.multiple_of(i * 8, 8)
+                for c, value in each(mm(w, g, left_h=True)):
+                    pair[pl.ds(row, 8), c * LANES : (c + 1) * LANES] = value
+
+        with jax.named_scope("products"):
+            for chunk in range(9):
+                columns = slice(chunk * 256, (chunk + 1) * 256)
+                high, low = split(pair[:, columns])
+                halves[0:64, columns] = high
+                halves[64:128, columns] = low
+                halves[128:192, columns] = high
+            weights = lax.dot_general(
+                halves[0:128, :], z[0:160, :], (((1,), (1,)), ((), ())), preferred_element_type=jnp.float32
+            )
+            half = weights[0:64] + weights[64:128]
+            half = half[:, 0:80] + half[:, 80:160]
+            sums.append(half[:, 8 * p : 8 * p + 64])
+            if p == 1:
+                both = sums[0] + sums[1]
+                both = jnp.concatenate([both[0:32], both[32:64]], axis=1)
+                for d in range(4):
+                    partial[d] = both[d * 8 : d * 8 + 8]
+                share_copies, share_arrivals = deal(partial, shares, share_send, share_recv)
+                for copy in share_copies:
+                    copy.start()
+                shares[here] = partial[here]
+                started += share_copies
+            for chunk in range(9):
+                columns = slice(chunk * 256, (chunk + 1) * 256)
+                value = jnp.dot(wt3[p], halves[:, columns], preferred_element_type=jnp.float32)
+                line[:, columns] = value if p == 0 else line[:, columns] + value
+        if p == 0:
+            direct(0)
 
     for r in range(8):
         final[r * 40 + 32 : r * 40 + 40, :] = jnp.zeros((8, LANES), jnp.float32)
@@ -420,29 +484,8 @@
         (0, slice(0, 16), back_send, back_recv),
         (1, slice(16, 40), last_send, last_recv),
     ):
-        with jax.named_scope("direct"):
-            @pl.loop(0, 3)
-            def _(a):
-                sums = [[None, None] for _ in range(3)]
-                for i in range(8):
-                    lines = slice(p * 64 + i * 8, p * 64 + i * 8 + 8)
-                    for k in range(3):
-                        at = (a * 3 + k) * 2
-                        gr = jnp.broadcast_to(cot[at, p, i : i + 1, :], (8, LANES))
-                        gi = jnp.broadcast_to(cot[at + 1, p, i : i + 1, :], (8, LANES))
-                        for b in range(3):
-                            at = comp(0, b, k) * LANES
-                            mr = mixed[lines, at : at + LANES]
-                            at = comp(1, b, k) * LANES
-                            mi = mixed[lines, at : at + LANES]
-                            re = gr * mr + gi * mi
-                            im = gi * mr - gr * mi
-                            s = sums[b]
-                            sums[b] = [re, im] if s[0] is None else [s[0] + re, s[1] + im]
-                for b in range(3):
-                    total[(a * 3 + b) * 2, p] = sums[b][0]
-                    total[(a * 3 + b) * 2 + 1, p] = sums[b][1]
-
+        if p == 1:
+            direct(1)
         with jax.named_scope("from_frame"):
             near, far = {}, {}
             for c in range(18):
@@ -474,40 +517,38 @@
             back_arrivals.append((rows, incoming))
             returned[me, rows, :] = back[me, rows, :]
 
-        if p == 0:
-            with jax.named_scope("share_sum"):
-                for arrival in share_arrivals:
-                    arrival.wait_recv()
-                subtotal = shares[0]
-                for s in range(1, 8):
-                    subtotal = subtotal + shares[s]
-                mine[...] = subtotal
-                across_copies, across_arrivals = spread(
-                    "yz", yz_count, mine, across, across_send, across_recv
-                )
-                for copy in across_copies:
-                    copy.start()
-                across[here] = subtotal
-                started += across_copies
-
-    with jax.named_scope("weight_sum"):
-        for arrival in across_arrivals:
+    with jax.named_scope("share_sum"):
+        for arrival in share_arrivals:
             arrival.wait_recv()
-        summed = across[0]
+        subtotal = shares[0]
         for s in range(1, yz_count):
-            summed = summed + across[s]
-        whole[me] = summed * scale
-        whole_copies, whole_arrivals = spread("gx", 8, whole.at[me], whole, whole_send, whole_recv)
-        for copy in whole_copies:
+            subtotal = subtotal + shares[s]
+        mine[...] = subtotal
+        across_copies, across_arrivals = spread("gx", 8, mine, across, across_send, across_recv)
+        for copy in across_copies:
             copy.start()
-        started += whole_copies
+        across[me] = subtotal
+        started += across_copies
 
     with jax.named_scope("unpack"):
-        for rows, incoming in back_arrivals:
+        for p, (rows, incoming) in enumerate(back_arrivals):
             for arrival in incoming:
                 arrival.wait_recv()
             for c, value in enumerate(block_transpose([returned[r, rows, :] for r in range(8)])):
                 out_ref[c, rows, :] = value
+            if p == 0:
+                for arrival in across_arrivals:
+                    arrival.wait_recv()
+                summed = across[0]
+                for s in range(1, 8):
+                    summed = summed + across[s]
+                whole[here] = summed * scale
+                whole_copies, whole_arrivals = spread(
+                    "yz", yz_count, whole.at[here], whole, whole_send, whole_recv
+                )
+                for copy in whole_copies:
+                    copy.start()
+                started += whole_copies
         for arrival in whole_arrivals:
             arrival.wait_recv()
         gw_out[...] = whole[...]
@@ -521,9 +562,10 @@
             row = x * 18 + ab * 2
             out_ref[:, x, ab // 3, ab % 3, :, :] = rows_ref[:, row : row + 2, :]
     for i in range(8):
-        value = weights_ref[i]
+        value = weights_ref[i % 4]
         for l in range(8):
-            gw_out[pl.ds(i * 64 + l, 8, stride=8), :] = value[:, l * 8 : l * 8 + 8]
+            at = i // 4 * 64 + l * 8
+            gw_out[pl.ds(i * 64 + l, 8, stride=8), :] = value[:, at : at + 8]
 
 
 def resident(scale, yz_count, gauge_links, in_field, cotangent, bilinear_weights):
@@ -535,7 +577,7 @@
         functools.partial(whole_kernel, scale, yz_count),
         out_shape=(
             jax.ShapeDtypeStruct((8, 40, LANES), f32),
-            jax.ShapeDtypeStruct((8, 8, LANES), f32),
+            jax.ShapeDtypeStruct((yz_count, 8, LANES), f32),
         ),
         in_specs=[placed] * 4,
         out_specs=(vmem, vmem),
@@ -555,22 +597,25 @@
             pltpu.VMEM((18, 2, 8, LANES), f32),
             pltpu.VMEM((128, 256), f32),
             pltpu.VMEM((256, 18 * LANES), jnp.bfloat16),
-            pltpu.VMEM((128, 18 * LANES), f32),
-            pltpu.VMEM((384, 18 * LANES), jnp.bfloat16),
+            pltpu.VMEM((64, 18 * LANES), f32),
+            pltpu.VMEM((192, 18 * LANES), jnp.bfloat16),
             pltpu.VMEM((128, 18 * LANES), f32),
             pltpu.VMEM((80, 18 * LANES), f32),
             pltpu.VMEM((18, 2, 8, LANES), f32),
             pltpu.VMEM((320, LANES), f32),
             pltpu.VMEM((8, 40, LANES), f32),
             pltpu.VMEM((8, 40, LANES), f32),
+            pltpu.VMEM((yz_count, 8, LANES), f32),
+            pltpu.VMEM((yz_count, 8, LANES), f32),
+            pltpu.VMEM((8, LANES), f32),
             pltpu.VMEM((8, 8, LANES), f32),
-            pltpu.VMEM((8, 8, LANES), f32),
-            pltpu.VMEM((8, LANES), f32),
             pltpu.VMEM((yz_count, 8, LANES), f32),
-            pltpu.VMEM((8, 8, LANES), f32),
         ]
         + [dma((8,))] * 10
-        + [dma((yz_count,)), dma((yz_count,)), dma((8,)), dma((8,)), dma((4,))],
+        + [dma((yz_count,))] * 2
+        + [dma((8,))] * 2
+        + [dma((yz_count,))] * 2
+        + [dma((4,))],
         compiler_params=pltpu.CompilerParams(
             collective_id=0, has_side_effects=True, vmem_limit_bytes=VMEM_BYTES
         ),
@@ -661,6 +706,7 @@
     yz = lax.axis_size("yz")
     fits = (
         gx == 8
+        and yz == 4
         and in_field.shape == (8, 2, 2, 3, 3, LANES)
         and bilinear_weights.shape == (8, 8, 8, 8)
     )

time: 28.6 us -> 30.5 us (1.066)
  Pallas kernels: 27.9 us -> 29.7 us
    pallas_call x1, Pallas kernels: 27 us -> 28.8 us  [resident(): pl.pallas_call(functools.partial(whole_kernel, scale, yz_count), out_shap...]
where the time goes in v4:
time: 30.5 us; the launch traced here: 30.3 us
  Pallas kernels  29.7 us (97%)
  between operations  0.64 us (2%)
    pallas_call x1, Pallas kernels, resident(): pl.pallas_call(functools.partial(whole_kernel, scale, yz_count), out_shap...  28.8 us
    pallas_call x1, Pallas kernels, resident(): pl.pallas_call(place_kernel, out_shape=(jax.ShapeDtypeStruct((8, 2, 3, 3,...  0.83 us

profile of v4, /device:TPU:0, one launch (start us, length us, event | category | flops | bytes accessed | tf_op | source)
XLA Modules:
  0.0 30.3 jit_solution(9779229714468441512)
XLA Ops:
  0.6 28.8 %lattice_backward.1 = (f32[8,40,128]{2,1,0:T(8,128)S(1)}, f32[4,8,128]{2,1,0:T(8,128)S(1)}) custom-call(f32[2,3,3,2,128]{4,3,2,1,0:T(2,128)} %bitcast.9, f32[8,2,3,3,2,128]{5,4,3,2,1,0:T(2,128)} %bitcast.7, f32[8,2,3,3,2,128]{5,4,3,2,1,0:T(2,128)} %bitcast.8, f32[512,8]{1,0:T(8,128)} %bitcast.6), custom_call_target="tpu_custom_call" | custom-call | tf_op jit(solution)/shard_map/lattice_backward/pallas_call | solution.py:576
  29.5 0.8 %place_rows.1 = (f32[8,2,3,3,2,128]{5,4,3,2,1,0:T(2,128)}, f32[512,8]{1,0:T(8,128)}) custom-call(f32[8,40,128]{2,1,0:T(8,128)S(1)} %get-tuple-element.6.rows_ref, f32[4,8,128]{2,1,0:T(8,128)S(1)} %get-tuple-element.7.weights_ref), custom_call_target="tpu_custom_call" | custom-call | tf_op jit(solution)/shard_map/place_rows/pallas_call | solution.py:629

commit v5 on v4

--- a/solution.py
+++ b/solution.py
@@ -183,25 +183,6 @@
                     send_sem=send_sem.at[k],
                     recv_sem=recv_sem.at[k],
                     device_id={"gx": peer},
-                    device_id_type=MESH,
-                )
-            )
-    return outgoing, incoming
-
-
-def deal(source, target, send_sem, recv_sem):
-    me = lax.axis_index("yz")
-    outgoing, incoming = [], []
-    for k in range(1, 4):
-        peer = other(me, k)
-        for found, slot in ((outgoing, me), (incoming, peer)):
-            found.append(
-                pltpu.make_async_remote_copy(
-                    src_ref=source.at[peer],
-                    dst_ref=target.at[slot],
-                    send_sem=send_sem.at[k],
-                    recv_sem=recv_sem.at[k],
-                    device_id={"yz": peer},
                     device_id_type=MESH,
                 )
             )
@@ -427,7 +408,6 @@
             columns = slice(chunk * 256, (chunk + 1) * 256)
             mixed[:, columns] = jnp.dot(w3, z[:, columns], preferred_element_type=jnp.float32)
 
-    sums = []
     for p, rows in ((0, even), (1, odd_part)):
         with jax.named_scope("pairs"):
             for arrival in arrivals[1 + p]:
@@ -448,31 +428,35 @@
                     pair[pl.ds(row, 8), c * LANES : (c + 1) * LANES] = value
 
         with jax.named_scope("products"):
+            base = p * 192
             for chunk in range(9):
                 columns = slice(chunk * 256, (chunk + 1) * 256)
                 high, low = split(pair[:, columns])
-                halves[0:64, columns] = high
-                halves[64:128, columns] = low
-                halves[128:192, columns] = high
-            weights = lax.dot_general(
-                halves[0:128, :], z[0:160, :], (((1,), (1,)), ((), ())), preferred_element_type=jnp.float32
-            )
-            half = weights[0:64] + weights[64:128]
-            half = half[:, 0:80] + half[:, 80:160]
-            sums.append(half[:, 8 * p : 8 * p + 64])
+                halves[base : base + 64, columns] = high
+                halves[base + 64 : base + 128, columns] = low
+                halves[base + 128 : base + 192, columns] = high
             if p == 1:
-                both = sums[0] + sums[1]
-                both = jnp.concatenate([both[0:32], both[32:64]], axis=1)
-                for d in range(4):
+                weights = lax.dot_general(
+                    jnp.concatenate([halves[0:128, :], halves[192:320, :]], axis=0),
+                    z[0:160, :],
+                    (((1,), (1,)), ((), ())),
+                    preferred_element_type=jnp.float32,
+                )
+                half = weights[:, 0:80] + weights[:, 80:160]
+                both = half[0:64, 0:64] + half[64:128, 0:64] + half[128:192, 8:72] + half[192:256, 8:72]
+                both = jnp.concatenate([both, jnp.zeros((64, 64), jnp.float32)], axis=1)
+                for d in range(8):
                     partial[d] = both[d * 8 : d * 8 + 8]
-                share_copies, share_arrivals = deal(partial, shares, share_send, share_recv)
+                share_copies, share_arrivals = exchange(
+                    partial, shares, slice(0, 8), share_send, share_recv
+                )
                 for copy in share_copies:
                     copy.start()
-                shares[here] = partial[here]
+                shares[me] = partial[me]
                 started += share_copies
             for chunk in range(9):
                 columns = slice(chunk * 256, (chunk + 1) * 256)
-                value = jnp.dot(wt3[p], halves[:, columns], preferred_element_type=jnp.float32)
+                value = jnp.dot(wt3[p], halves[base : base + 192, columns], preferred_element_type=jnp.float32)
                 line[:, columns] = value if p == 0 else line[:, columns] + value
         if p == 0:
             direct(0)
@@ -517,18 +501,33 @@
             back_arrivals.append((rows, incoming))
             returned[me, rows, :] = back[me, rows, :]
 
-    with jax.named_scope("share_sum"):
-        for arrival in share_arrivals:
+        if p == 0:
+            with jax.named_scope("share_sum"):
+                for arrival in share_arrivals:
+                    arrival.wait_recv()
+                subtotal = shares[0]
+                for s in range(1, 8):
+                    subtotal = subtotal + shares[s]
+                mine[...] = subtotal
+                across_copies, across_arrivals = spread(
+                    "yz", yz_count, mine, across, across_send, across_recv
+                )
+                for copy in across_copies:
+                    copy.start()
+                across[here] = subtotal
+                started += across_copies
+
+    with jax.named_scope("weight_sum"):
+        for arrival in across_arrivals:
             arrival.wait_recv()
-        subtotal = shares[0]
+        summed = across[0]
         for s in range(1, yz_count):
-            subtotal = subtotal + shares[s]
-        mine[...] = subtotal
-        across_copies, across_arrivals = spread("gx", 8, mine, across, across_send, across_recv)
-        for copy in across_copies:
+            summed = summed + across[s]
+        whole[me] = summed * scale
+        whole_copies, whole_arrivals = spread("gx", 8, whole.at[me], whole, whole_send, whole_recv)
+        for copy in whole_copies:
             copy.start()
-        across[me] = subtotal
-        started += across_copies
+        started += whole_copies
 
     with jax.named_scope("unpack"):
         for p, (rows, incoming) in enumerate(back_arrivals):
@@ -536,19 +535,6 @@
                 arrival.wait_recv()
             for c, value in enumerate(block_transpose([returned[r, rows, :] for r in range(8)])):
                 out_ref[c, rows, :] = value
-            if p == 0:
-                for arrival in across_arrivals:
-                    arrival.wait_recv()
-                summed = across[0]
-                for s in range(1, 8):
-                    summed = summed + across[s]
-                whole[here] = summed * scale
-                whole_copies, whole_arrivals = spread(
-                    "yz", yz_count, whole.at[here], whole, whole_send, whole_recv
-                )
-                for copy in whole_copies:
-                    copy.start()
-                started += whole_copies
         for arrival in whole_arrivals:
             arrival.wait_recv()
         gw_out[...] = whole[...]
@@ -562,10 +548,9 @@
             row = x * 18 + ab * 2
             out_ref[:, x, ab // 3, ab % 3, :, :] = rows_ref[:, row : row + 2, :]
     for i in range(8):
-        value = weights_ref[i % 4]
+        value = weights_ref[i]
         for l in range(8):
-            at = i // 4 * 64 + l * 8
-            gw_out[pl.ds(i * 64 + l, 8, stride=8), :] = value[:, at : at + 8]
+            gw_out[pl.ds(i * 64 + l, 8, stride=8), :] = value[:, l * 8 : l * 8 + 8]
 
 
 def resident(scale, yz_count, gauge_links, in_field, cotangent, bilinear_weights):
@@ -577,7 +562,7 @@
         functools.partial(whole_kernel, scale, yz_count),
         out_shape=(
             jax.ShapeDtypeStruct((8, 40, LANES), f32),
-            jax.ShapeDtypeStruct((yz_count, 8, LANES), f32),
+            jax.ShapeDtypeStruct((8, 8, LANES), f32),
         ),
         in_specs=[placed] * 4,
         out_specs=(vmem, vmem),
@@ -598,23 +583,22 @@
             pltpu.VMEM((128, 256), f32),
             pltpu.VMEM((256, 18 * LANES), jnp.bfloat16),
             pltpu.VMEM((64, 18 * LANES), f32),
-            pltpu.VMEM((192, 18 * LANES), jnp.bfloat16),
+            pltpu.VMEM((384, 18 * LANES), jnp.bfloat16),
             pltpu.VMEM((128, 18 * LANES), f32),
             pltpu.VMEM((80, 18 * LANES), f32),
             pltpu.VMEM((18, 2, 8, LANES), f32),
             pltpu.VMEM((320, LANES), f32),
             pltpu.VMEM((8, 40, LANES), f32),
             pltpu.VMEM((8, 40, LANES), f32),
+            pltpu.VMEM((8, 8, LANES), f32),
+            pltpu.VMEM((8, 8, LANES), f32),
+            pltpu.VMEM((8, LANES), f32),
             pltpu.VMEM((yz_count, 8, LANES), f32),
-            pltpu.VMEM((yz_count, 8, LANES), f32),
-            pltpu.VMEM((8, LANES), f32),
             pltpu.VMEM((8, 8, LANES), f32),
-            pltpu.VMEM((yz_count, 8, LANES), f32),
         ]
-        + [dma((8,))] * 10
+        + [dma((8,))] * 12
         + [dma((yz_count,))] * 2
         + [dma((8,))] * 2
-        + [dma((yz_count,))] * 2
         + [dma((4,))],
         compiler_params=pltpu.CompilerParams(
             collective_id=0, has_side_effects=True, vmem_limit_bytes=VMEM_BYTES
@@ -706,7 +690,6 @@
     yz = lax.axis_size("yz")
     fits = (
         gx == 8
-        and yz == 4
         and in_field.shape == (8, 2, 2, 3, 3, LANES)
         and bilinear_weights.shape == (8, 8, 8, 8)
     )

time: 30.5 us -> 29.1 us (0.954)
  Pallas kernels: 29.7 us -> 28.3 us
    pallas_call x1, Pallas kernels: 28.8 us -> 27.5 us  [resident(): pl.pallas_call(functools.partial(whole_kernel, scale, yz_count), out_shap...]
where the time goes in v5:
time: 29.1 us; the launch traced here: 29 us
  Pallas kernels  28.3 us (97%)
  between operations  0.64 us (2%)
    pallas_call x1, Pallas kernels, resident(): pl.pallas_call(functools.partial(whole_kernel, scale, yz_count), out_shap...  27.5 us
    pallas_call x1, Pallas kernels, resident(): pl.pallas_call(place_kernel, out_shape=(jax.ShapeDtypeStruct((8, 2, 3, 3,...  0.84 us

profile of v5, /device:TPU:0, one launch (start us, length us, event | category | flops | bytes accessed | tf_op | source)
XLA Modules:
  0.0 29.0 jit_solution(10407796619304173576)
XLA Ops:
  0.6 27.5 %lattice_backward.1 = (f32[8,40,128]{2,1,0:T(8,128)S(1)}, f32[8,8,128]{2,1,0:T(8,128)S(1)}) custom-call(f32[2,3,3,2,128]{4,3,2,1,0:T(2,128)} %bitcast.9, f32[8,2,3,3,2,128]{5,4,3,2,1,0:T(2,128)} %bitcast.7, f32[8,2,3,3,2,128]{5,4,3,2,1,0:T(2,128)} %bitcast.8, f32[512,8]{1,0:T(8,128)} %bitcast.6), custom_call_target="tpu_custom_call" | custom-call | tf_op jit(solution)/shard_map/lattice_backward/pallas_call | solution.py:561
  28.1 0.8 %place_rows.1 = (f32[8,2,3,3,2,128]{5,4,3,2,1,0:T(2,128)}, f32[512,8]{1,0:T(8,128)}) custom-call(f32[8,40,128]{2,1,0:T(8,128)S(1)} %get-tuple-element.6.rows_ref, f32[8,8,128]{2,1,0:T(8,128)S(1)} %get-tuple-element.7.weights_ref), custom_call_target="tpu_custom_call" | custom-call | tf_op jit(solution)/shard_map/place_rows/pallas_call | solution.py:613

commit v6 on v5

--- a/solution.py
+++ b/solution.py
@@ -127,47 +127,49 @@
     return arrays
 
 
-def greet(axes):
+def other(me, mask):
+    for bit in (1, 2, 4):
+        if mask & bit:
+            me = me + bit - 2 * bit * (me // bit % 2)
+    return me
+
+
+FAR_FIRST = (4, 5, 6, 7, 2, 3, 1)
+
+
+def everyone():
+    me, here = lax.axis_index("gx"), lax.axis_index("yz")
+    return [
+        (g * 4 + y, other(me, g), other(here, y))
+        for g in FAR_FIRST + (0,)
+        for y in (3, 1, 2, 0)
+        if g or y
+    ]
+
+
+def greet():
     barrier = pltpu.get_barrier_semaphore()
-    total = 0
-    for axis, count in axes:
-        me = lax.axis_index(axis)
-        for k in range(1, count):
-            peer = lax.rem(me + k, count)
-            pl.semaphore_signal(barrier, inc=1, device_id={axis: peer}, device_id_type=MESH)
-        total += count - 1
-    return lambda: pl.semaphore_wait(barrier, total)
-
-
-def spread(axis, count, source, target, send, recv):
-    at = lax.axis_index(axis)
+    for _, gx, yz in everyone():
+        pl.semaphore_signal(barrier, inc=1, device_id={"gx": gx, "yz": yz}, device_id_type=MESH)
+    return lambda: pl.semaphore_wait(barrier, 31)
+
+
+def spread(source, target, send, recv):
+    mine = lax.axis_index("gx") * 4 + lax.axis_index("yz")
     outgoing, incoming = [], []
-    for k in range(1, count):
-        for found, slot, there in (
-            (outgoing, at, lax.rem(at + k, count)),
-            (incoming, lax.rem(at + count - k, count), lax.rem(at + count - k, count)),
-        ):
+    for k, gx, yz in everyone():
+        for found, slot in ((outgoing, mine), (incoming, gx * 4 + yz)):
             found.append(
                 pltpu.make_async_remote_copy(
                     src_ref=source,
                     dst_ref=target.at[slot],
                     send_sem=send.at[k],
                     recv_sem=recv.at[k],
-                    device_id={axis: there},
+                    device_id={"gx": gx, "yz": yz},
                     device_id_type=MESH,
                 )
             )
     return outgoing, incoming
-
-
-def other(me, mask):
-    for bit in (1, 2, 4):
-        if mask & bit:
-            me = me + bit - 2 * bit * (me // bit % 2)
-    return me
-
-
-FAR_FIRST = (4, 5, 6, 7, 2, 3, 1)
 
 
 def exchange(source, target, rows, send_sem, recv_sem):
@@ -178,8 +180,8 @@
         for found, slot in ((outgoing, me), (incoming, peer)):
             found.append(
                 pltpu.make_async_remote_copy(
-                    src_ref=source.at[peer, rows, :],
-                    dst_ref=target.at[slot, rows, :],
+                    src_ref=source.at[peer, rows],
+                    dst_ref=target.at[slot, rows],
                     send_sem=send_sem.at[k],
                     recv_sem=recv_sem.at[k],
                     device_id={"gx": peer},
@@ -191,7 +193,6 @@
 
 def whole_kernel(
     scale,
-    yz_count,
     u_hbm,
     w_hbm,
     g_hbm,
@@ -225,7 +226,6 @@
     shares,
     mine,
     across,
-    whole,
     first_send,
     first_recv,
     second_send,
@@ -240,8 +240,6 @@
     share_recv,
     across_send,
     across_recv,
-    whole_send,
-    whole_recv,
     load_sem,
 ):
     me = lax.axis_index("gx")
@@ -254,7 +252,7 @@
     ]
     for load in loads:
         load.start()
-    ready = greet((("gx", 8), ("yz", yz_count)))
+    ready = greet()
     lane1 = lax.broadcasted_iota(jnp.int32, (1, LANES), 1)
     lane = lax.broadcasted_iota(jnp.int32, (8, LANES), 1)
     early, even, odd_part = slice(0, 48), slice(48, 64), slice(64, 80)
@@ -444,11 +442,12 @@
                 )
                 half = weights[:, 0:80] + weights[:, 80:160]
                 both = half[0:64, 0:64] + half[64:128, 0:64] + half[128:192, 8:72] + half[192:256, 8:72]
-                both = jnp.concatenate([both, jnp.zeros((64, 64), jnp.float32)], axis=1)
                 for d in range(8):
-                    partial[d] = both[d * 8 : d * 8 + 8]
+                    partial[d] = jnp.concatenate(
+                        [both[d * 8 : d * 8 + 4], both[d * 8 + 4 : d * 8 + 8]], axis=1
+                    )
                 share_copies, share_arrivals = exchange(
-                    partial, shares, slice(0, 8), share_send, share_recv
+                    partial, shares, slice(0, 4), share_send, share_recv
                 )
                 for copy in share_copies:
                     copy.start()
@@ -509,25 +508,11 @@
                 for s in range(1, 8):
                     subtotal = subtotal + shares[s]
                 mine[...] = subtotal
-                across_copies, across_arrivals = spread(
-                    "yz", yz_count, mine, across, across_send, across_recv
-                )
+                across_copies, across_arrivals = spread(mine, across, across_send, across_recv)
                 for copy in across_copies:
                     copy.start()
-                across[here] = subtotal
+                across[me * 4 + here] = subtotal
                 started += across_copies
-
-    with jax.named_scope("weight_sum"):
-        for arrival in across_arrivals:
-            arrival.wait_recv()
-        summed = across[0]
-        for s in range(1, yz_count):
-            summed = summed + across[s]
-        whole[me] = summed * scale
-        whole_copies, whole_arrivals = spread("gx", 8, whole.at[me], whole, whole_send, whole_recv)
-        for copy in whole_copies:
-            copy.start()
-        started += whole_copies
 
     with jax.named_scope("unpack"):
         for p, (rows, incoming) in enumerate(back_arrivals):
@@ -535,9 +520,13 @@
                 arrival.wait_recv()
             for c, value in enumerate(block_transpose([returned[r, rows, :] for r in range(8)])):
                 out_ref[c, rows, :] = value
-        for arrival in whole_arrivals:
+        for arrival in across_arrivals:
             arrival.wait_recv()
-        gw_out[...] = whole[...]
+        for d in range(8):
+            summed = across[d * 4]
+            for y in range(1, 4):
+                summed = summed + across[d * 4 + y]
+            gw_out[d] = summed * scale
         for copy in started:
             copy.wait_send()
 
@@ -549,20 +538,21 @@
             out_ref[:, x, ab // 3, ab % 3, :, :] = rows_ref[:, row : row + 2, :]
     for i in range(8):
         value = weights_ref[i]
+        value = jnp.concatenate([value[:, 0:64], value[:, 64:LANES]], axis=0)
         for l in range(8):
             gw_out[pl.ds(i * 64 + l, 8, stride=8), :] = value[:, l * 8 : l * 8 + 8]
 
 
-def resident(scale, yz_count, gauge_links, in_field, cotangent, bilinear_weights):
+def resident(scale, gauge_links, in_field, cotangent, bilinear_weights):
     f32 = jnp.float32
     vmem = pl.BlockSpec(memory_space=pltpu.VMEM)
     dma = pltpu.SemaphoreType.DMA
     placed = pl.BlockSpec(memory_space=pltpu.HBM)
     rows, weights = pl.pallas_call(
-        functools.partial(whole_kernel, scale, yz_count),
+        functools.partial(whole_kernel, scale),
         out_shape=(
             jax.ShapeDtypeStruct((8, 40, LANES), f32),
-            jax.ShapeDtypeStruct((8, 8, LANES), f32),
+            jax.ShapeDtypeStruct((8, 4, LANES), f32),
         ),
         in_specs=[placed] * 4,
         out_specs=(vmem, vmem),
@@ -590,15 +580,13 @@
             pltpu.VMEM((320, LANES), f32),
             pltpu.VMEM((8, 40, LANES), f32),
             pltpu.VMEM((8, 40, LANES), f32),
-            pltpu.VMEM((8, 8, LANES), f32),
-            pltpu.VMEM((8, 8, LANES), f32),
-            pltpu.VMEM((8, LANES), f32),
-            pltpu.VMEM((yz_count, 8, LANES), f32),
-            pltpu.VMEM((8, 8, LANES), f32),
+            pltpu.VMEM((8, 4, LANES), f32),
+            pltpu.VMEM((8, 4, LANES), f32),
+            pltpu.VMEM((4, LANES), f32),
+            pltpu.VMEM((32, 4, LANES), f32),
         ]
         + [dma((8,))] * 12
-        + [dma((yz_count,))] * 2
-        + [dma((8,))] * 2
+        + [dma((32,))] * 2
         + [dma((4,))],
         compiler_params=pltpu.CompilerParams(
             collective_id=0, has_side_effects=True, vmem_limit_bytes=VMEM_BYTES
@@ -690,6 +678,7 @@
     yz = lax.axis_size("yz")
     fits = (
         gx == 8
+        and yz == 4
         and in_field.shape == (8, 2, 2, 3, 3, LANES)
         and bilinear_weights.shape == (8, 8, 8, 8)
     )
@@ -697,7 +686,7 @@
         return general(gauge_links, in_field, cotangent, bilinear_weights)
     total = gauge_links.shape[0] * gx * gauge_links.shape[-1] * yz
     scale = 1.0 / math.sqrt(100.0 * total)
-    return resident(scale, yz, gauge_links, in_field, cotangent, bilinear_weights)
+    return resident(scale, gauge_links, in_field, cotangent, bilinear_weights)
 
 
 def solution(mesh):

time: 29.1 us -> 29.5 us (1.014)
  Pallas kernels: 28.3 us -> 28.7 us
    pallas_call x1, Pallas kernels: 27.5 us -> 27.8 us  [resident(): pl.pallas_call(functools.partial(whole_kernel, scale), out_shape=(jax.Sha...]
where the time goes in v6:
time: 29.5 us; the launch traced here: 29.4 us
  Pallas kernels  28.7 us (97%)
  between operations  0.64 us (2%)
    pallas_call x1, Pallas kernels, resident(): pl.pallas_call(functools.partial(whole_kernel, scale), out_shape=(jax.Sha...  27.8 us
    pallas_call x1, Pallas kernels, resident(): pl.pallas_call(place_kernel, out_shape=(jax.ShapeDtypeStruct((8, 2, 3, 3,...  0.9 us

profile of v6, /device:TPU:0, one launch (start us, length us, event | category | flops | bytes accessed | tf_op | source)
XLA Modules:
  0.0 29.4 jit_solution(14028130192264610789)
XLA Ops:
  0.6 27.8 %lattice_backward.1 = (f32[8,40,128]{2,1,0:T(8,128)S(1)}, f32[8,4,128]{2,1,0:T(4,128)S(1)}) custom-call(f32[2,3,3,2,128]{4,3,2,1,0:T(2,128)} %bitcast.9, f32[8,2,3,3,2,128]{5,4,3,2,1,0:T(2,128)} %bitcast.7, f32[8,2,3,3,2,128]{5,4,3,2,1,0:T(2,128)} %bitcast.8, f32[512,8]{1,0:T(8,128)} %bitcast.6), custom_call_target="tpu_custom_call" | custom-call | tf_op jit(solution)/shard_map/lattice_backward/pallas_call | solution.py:551
  28.5 0.9 %place_rows.1 = (f32[8,2,3,3,2,128]{5,4,3,2,1,0:T(2,128)}, f32[512,8]{1,0:T(8,128)}) custom-call(f32[8,40,128]{2,1,0:T(8,128)S(1)} %get-tuple-element.6.rows_ref, f32[8,4,128]{2,1,0:T(4,128)S(1)} %get-tuple-element.7.weights_ref), custom_call_target="tpu_custom_call" | custom-call | tf_op jit(solution)/shard_map/place_rows/pallas_call | solution.py:601

commit v7 on v5

--- a/solution.py
+++ b/solution.py
@@ -257,25 +257,20 @@
     ready = greet((("gx", 8), ("yz", yz_count)))
     lane1 = lax.broadcasted_iota(jnp.int32, (1, LANES), 1)
     lane = lax.broadcasted_iota(jnp.int32, (8, LANES), 1)
-    early, even, odd_part = slice(0, 48), slice(48, 64), slice(64, 80)
+    early, even, odd_part = slice(0, 40), slice(40, 64), slice(64, 80)
 
     with jax.named_scope("pack"):
-        packed[:, 32:48, :] = jnp.zeros((8, 16, LANES), jnp.float32)
-        packed[:, 72:80, :] = jnp.zeros((8, 8, LANES), jnp.float32)
         loads[0].wait()
         loads[1].wait()
         for x in range(2):
             for ab in range(9):
                 row = x * 18 + ab * 2
                 packed[:, row : row + 2, :] = w_ref[:, x, ab // 3, ab % 3, :, :]
+                if ab == 8:
+                    continue
                 for part in range(2):
-                    r, t = divmod(row + part, 5)
+                    r, t = divmod(x * 16 + ab * 2 + part, 4)
                     packed[r, 36 + t : 37 + t, :] = u_ref[x, ab // 3, ab % 3, part : part + 1, :]
-        loads[2].wait()
-        for x in range(2):
-            for ab in range(9):
-                row = x * 18 + ab * 2
-                packed[:, 41 + row : 43 + row, :] = g_ref[:, x, ab // 3, ab % 3, :, :]
         started = []
         arrivals = []
         for rows, send, recv in (
@@ -283,6 +278,13 @@
             (even, second_send, second_recv),
             (odd_part, third_send, third_recv),
         ):
+            if rows is even:
+                loads[2].wait()
+                packed[:, 72:80, :] = jnp.zeros((8, 8, LANES), jnp.float32)
+                for x in range(2):
+                    for ab in range(9):
+                        row = 40 + x * 18 + ab * 2
+                        packed[:, row : row + 2, :] = g_ref[:, x, ab // 3, ab % 3, :, :]
             for d, value in enumerate(block_transpose([packed[r, rows, :] for r in range(8)])):
                 sending[d, rows, :] = value
             if not started:
@@ -319,14 +321,23 @@
         for arrival in arrivals[0]:
             arrival.wait_recv()
         for c, value in enumerate(block_transpose([landed[r, early, :] for r in range(8)])):
-            sites[c * 80 : c * 80 + 48, :] = value
-
-        def link(p, c):
-            r, t = divmod(p * 18 + c, 5)
-            return sites[r * 80 + 36 + t : r * 80 + 37 + t, :]
-
-        u0 = read_matrix(lambda c: link(0, c))
-        u1 = read_matrix(lambda c: link(1, c))
+            sites[c * 80 : c * 80 + 40, :] = value
+
+        def link(p):
+            def read(c):
+                if c >= 16:
+                    return None
+                r, t = divmod(p * 16 + c, 4)
+                return sites[r * 80 + 36 + t : r * 80 + 37 + t, :]
+
+            m = read_matrix(read)
+            re, im = m
+            re[2][2] = re[0][0] * re[1][1] - im[0][0] * im[1][1] - re[0][1] * re[1][0] + im[0][1] * im[1][0]
+            im[2][2] = re[0][1] * im[1][0] + im[0][1] * re[1][0] - re[0][0] * im[1][1] - im[0][0] * re[1][1]
+            return m
+
+        u0 = link(0)
+        u1 = link(1)
         one = [[[jnp.float32(1.0 if r == 0 and a == b else 0.0) for b in range(3)] for a in range(3)] for r in range(2)]
         prefix = mm(u0, u1)
         for step in (1, 2, 4):
@@ -415,7 +426,7 @@
             for c, value in enumerate(block_transpose([landed[r, rows, :] for r in range(8)])):
                 sites[c * 80 + rows.start : c * 80 + rows.stop, :] = value
             v = read_matrix(lambda c: v_all[c, p])
-            g = read_matrix(lambda c: sites[pl.ds(41 + p * 18 + c, 8, stride=80), :])
+            g = read_matrix(lambda c: sites[pl.ds(40 + p * 18 + c, 8, stride=80), :])
             for c, value in each(conjugate_by(v, g)):
                 cot[c, p] = value
 

time: 29.1 us -> 28.7 us (0.986)
  Pallas kernels: 28.3 us -> 28 us
    pallas_call x1, Pallas kernels: 27.5 us -> 27.1 us  [resident(): pl.pallas_call(functools.partial(whole_kernel, scale, yz_count), out_shap...]
where the time goes in v7:
time: 28.7 us; the launch traced here: 28.6 us
  Pallas kernels  28 us (98%)
  between operations  0.64 us (2%)
    pallas_call x1, Pallas kernels, resident(): pl.pallas_call(functools.partial(whole_kernel, scale, yz_count), out_shap...  27.1 us
    pallas_call x1, Pallas kernels, resident(): pl.pallas_call(place_kernel, out_shape=(jax.ShapeDtypeStruct((8, 2, 3, 3,...  0.84 us

profile of v7, /device:TPU:0, one launch (start us, length us, event | category | flops | bytes accessed | tf_op | source)
XLA Modules:
  0.0 28.6 jit_solution(553145683579258956)
XLA Ops:
  0.6 27.1 %lattice_backward.1 = (f32[8,40,128]{2,1,0:T(8,128)S(1)}, f32[8,8,128]{2,1,0:T(8,128)S(1)}) custom-call(f32[2,3,3,2,128]{4,3,2,1,0:T(2,128)} %bitcast.9, f32[8,2,3,3,2,128]{5,4,3,2,1,0:T(2,128)} %bitcast.7, f32[8,2,3,3,2,128]{5,4,3,2,1,0:T(2,128)} %bitcast.8, f32[512,8]{1,0:T(8,128)} %bitcast.6), custom_call_target="tpu_custom_call" | custom-call | tf_op jit(solution)/shard_map/lattice_backward/pallas_call | solution.py:572
  27.8 0.8 %place_rows.1 = (f32[8,2,3,3,2,128]{5,4,3,2,1,0:T(2,128)}, f32[512,8]{1,0:T(8,128)}) custom-call(f32[8,40,128]{2,1,0:T(8,128)S(1)} %get-tuple-element.6.rows_ref, f32[8,8,128]{2,1,0:T(8,128)S(1)} %get-tuple-element.7.weights_ref), custom_call_target="tpu_custom_call" | custom-call | tf_op jit(solution)/shard_map/place_rows/pallas_call | solution.py:624

commit v8 on v7

--- a/solution.py
+++ b/solution.py
@@ -257,7 +257,7 @@
     ready = greet((("gx", 8), ("yz", yz_count)))
     lane1 = lax.broadcasted_iota(jnp.int32, (1, LANES), 1)
     lane = lax.broadcasted_iota(jnp.int32, (8, LANES), 1)
-    early, even, odd_part = slice(0, 40), slice(40, 64), slice(64, 80)
+    early, even, odd_part = slice(0, 40), slice(40, 64), slice(64, 76)
 
     with jax.named_scope("pack"):
         loads[0].wait()
@@ -280,7 +280,6 @@
         ):
             if rows is even:
                 loads[2].wait()
-                packed[:, 72:80, :] = jnp.zeros((8, 8, LANES), jnp.float32)
                 for x in range(2):
                     for ab in range(9):
                         row = 40 + x * 18 + ab * 2
@@ -472,12 +471,10 @@
         if p == 0:
             direct(0)
 
-    for r in range(8):
-        final[r * 40 + 32 : r * 40 + 40, :] = jnp.zeros((8, LANES), jnp.float32)
     back_arrivals = []
     for p, rows, send, recv in (
         (0, slice(0, 16), back_send, back_recv),
-        (1, slice(16, 40), last_send, last_recv),
+        (1, slice(16, 36), last_send, last_recv),
     ):
         if p == 1:
             direct(1)
@@ -572,7 +569,7 @@
     rows, weights = pl.pallas_call(
         functools.partial(whole_kernel, scale, yz_count),
         out_shape=(
-            jax.ShapeDtypeStruct((8, 40, LANES), f32),
+            jax.ShapeDtypeStruct((8, 36, LANES), f32),
             jax.ShapeDtypeStruct((8, 8, LANES), f32),
         ),
         in_specs=[placed] * 4,
@@ -583,8 +580,8 @@
             pltpu.VMEM((8, 2, 3, 3, 2, LANES), f32),
             pltpu.VMEM((512, 8), f32),
             pltpu.VMEM((8, 80, LANES), f32),
-            pltpu.VMEM((8, 80, LANES), f32),
-            pltpu.VMEM((8, 80, LANES), f32),
+            pltpu.VMEM((8, 76, LANES), f32),
+            pltpu.VMEM((8, 76, LANES), f32),
             pltpu.VMEM((640, LANES), f32),
             pltpu.VMEM((18, 2, 8, LANES), f32),
             pltpu.VMEM((18, 2, 8, LANES), f32),
@@ -599,8 +596,8 @@
             pltpu.VMEM((80, 18 * LANES), f32),
             pltpu.VMEM((18, 2, 8, LANES), f32),
             pltpu.VMEM((320, LANES), f32),
-            pltpu.VMEM((8, 40, LANES), f32),
-            pltpu.VMEM((8, 40, LANES), f32),
+            pltpu.VMEM((8, 36, LANES), f32),
+            pltpu.VMEM((8, 36, LANES), f32),
             pltpu.VMEM((8, 8, LANES), f32),
             pltpu.VMEM((8, 8, LANES), f32),
             pltpu.VMEM((8, LANES), f32),

time: 28.7 us -> 28.6 us (level)
  no operation moved by 1% of the time
where the time goes in v8:
time: 28.6 us; the launch traced here: 28.4 us
  Pallas kernels  27.8 us (97%)
  between operations  0.64 us (2%)
    pallas_call x1, Pallas kernels, resident(): pl.pallas_call(functools.partial(whole_kernel, scale, yz_count), out_shap...  27 us
    pallas_call x1, Pallas kernels, resident(): pl.pallas_call(place_kernel, out_shape=(jax.ShapeDtypeStruct((8, 2, 3, 3,...  0.84 us

profile of v8, /device:TPU:0, one launch (start us, length us, event | category | flops | bytes accessed | tf_op | source)
XLA Modules:
  0.0 28.4 jit_solution(16168741572517014177)
XLA Ops:
  0.6 27.0 %lattice_backward.1 = (f32[8,36,128]{2,1,0:T(8,128)S(1)}, f32[8,8,128]{2,1,0:T(8,128)S(1)}) custom-call(f32[2,3,3,2,128]{4,3,2,1,0:T(2,128)} %bitcast.9, f32[8,2,3,3,2,128]{5,4,3,2,1,0:T(2,128)} %bitcast.7, f32[8,2,3,3,2,128]{5,4,3,2,1,0:T(2,128)} %bitcast.8, f32[512,8]{1,0:T(8,128)} %bitcast.6), custom_call_target="tpu_custom_call" | custom-call | tf_op jit(solution)/shard_map/lattice_backward/pallas_call | solution.py:569
  27.6 0.8 %place_rows.1 = (f32[8,2,3,3,2,128]{5,4,3,2,1,0:T(2,128)}, f32[512,8]{1,0:T(8,128)}) custom-call(f32[8,36,128]{2,1,0:T(8,128)S(1)} %get-tuple-element.6.rows_ref, f32[8,8,128]{2,1,0:T(8,128)S(1)} %get-tuple-element.7.weights_ref), custom_call_target="tpu_custom_call" | custom-call | tf_op jit(solution)/shard_map/place_rows/pallas_call | solution.py:621
